TPU v7x, 128 devices: a whole 4x4x4 slice. The times are simulated.
128 devices in a mesh: rows: 128 (over z, x, y, core).
Axes of the slice: x: 4, y: 4, z: 4, core: 2. Of those that a mesh axis runs over, the one named last changes fastest.
Arguments:
- matrix: float32 [2097152, 128], P('rows'), may hold values from -60 to 60, as said below
- signs: int32 [2097152], P('rows'), may hold values from -1 to 1, as said below
- sample_rows: int32 [32768], P('rows'), may hold values from 0 to 2097151, as said below
Outputs:
- sketch: float32 [32768, 128], P('rows')
- r_factors: float32 [16, 128, 128], replicated
Inputs may be any that keep to these rules, and one draw needn't show every extreme that they name: `matrix`: every entry is finite. `signs`: every entry is -1 or 1. `sample_rows`: entries are ascending within each device's 2 entries from one source range, and each block of 256 entries (one device's share) takes exactly 2 entries from each device's range of 16384 matrix rows, in device order; within such a block, exactly 2 entries have an offset inside their range (index modulo 16384) in each of the 128 aligned offset intervals of length 128; repeats may occur.
All inputs are finite; a program needn't handle non-finite values.
Results may differ from a plain program's by a relative error of at most 0.00013.
Values sent between devices are 32-bit elements; how exact they have to be, the bound alone decides.
A program may use at most 128 MiB of HBM per device.

v0:
```python
import math

import jax
import jax.numpy as jnp
from jax import lax
from jax.sharding import PartitionSpec as P

SAMP_OWN = 2048


highest = lax.Precision.HIGHEST


def swapped(value, axis, stride):
    mask = 2**stride
    pairs = [(source, source ^ mask) for source in range(lax.axis_size(axis))]
    return lax.ppermute(value, axis, pairs)


def sylvester(order):
    first = jnp.arange(order, dtype=jnp.int32)[:, None]
    second = jnp.arange(order, dtype=jnp.int32)[None, :]
    common = jnp.bitwise_and(first, second)
    parity = jnp.zeros((order, order), jnp.int32)
    for bit_index in range(order.bit_length() - 1):
        parity = parity + jnp.bitwise_and(jnp.right_shift(common, bit_index), 1)
    return (1 - 2 * (parity % 2)).astype(jnp.float32)


def local_transform(field):
    rows_dev, width = field.shape
    inner = min(2048, rows_dev)
    outer = rows_dev // inner
    blocks = field.reshape(outer, inner, width)
    blocks = jnp.einsum("ij,ajc->aic", sylvester(inner), blocks, precision=highest)
    blocks = jnp.einsum("ab,bic->aic", sylvester(outer), blocks, precision=highest)
    return blocks.reshape(rows_dev, width)


def body(matrix, signs, sample_rows):
    rows_dev, width = matrix.shape
    dev_count = lax.axis_size("rows")
    total = rows_dev * dev_count
    field = matrix * signs.astype(jnp.float32)[:, None] * (1.0 / math.sqrt(total))
    field = local_transform(field)
    per_source = sample_rows.shape[0] // dev_count
    order = jnp.arange(sample_rows.shape[0], dtype=jnp.int32)
    pick_index = sample_rows % rows_dev
    my_index = lax.axis_index("rows")
    source = field
    for bit_index in range(dev_count.bit_length() - 1):
        partner = swapped(source, "rows", bit_index)
        upper = jnp.bitwise_and(jnp.right_shift(my_index, bit_index), 1) == 1
        source = jnp.where(upper, partner - source, source + partner)
    wanted = pick_index.reshape(dev_count, per_source)
    requested = lax.all_to_all(wanted, "rows", split_axis=0, concat_axis=0, tiled=True)
    chosen = jnp.take(source, requested.reshape(-1), axis=0).reshape(
        requested.shape[0], requested.shape[1], width
    )
    arrived = lax.all_to_all(chosen, "rows", split_axis=0, concat_axis=0, tiled=True).reshape(
        -1, width
    )
    sketch = jnp.zeros_like(arrived).at[order].set(arrived)
    partial_gram = jnp.einsum("sc,sd->cd", sketch, sketch, precision=highest)
    group_size = SAMP_OWN // sample_rows.shape[0]
    owner_count = dev_count // group_size
    my_group = lax.axis_index("rows") // group_size
    slot_mask = (jnp.arange(owner_count, dtype=jnp.int32) == my_group).astype(jnp.float32)[
        :, None, None
    ]
    grams = lax.psum(slot_mask * partial_gram[None], "rows")
    lower = jnp.linalg.cholesky(grams / SAMP_OWN)
    return (sketch, jnp.swapaxes(lower, 1, 2))


def solution(mesh):
    return jax.shard_map(
        body,
        mesh=mesh,
        in_specs=(P("rows", None), P("rows"), P("rows")),
        out_specs=(P("rows", None), P()),
        check_vma=False,
    )
```

profile of v0, /device:TPU:1, one launch (start us, length us, event | category | flops | bytes accessed | tf_op | source)
XLA Modules:
  0.0 1751.8 jit_solution(2294181306608433864)
XLA Ops:
  7.2 0.0 copy-start.2
  7.2 0.0 copy-start
  7.2 25.2 %fusion.63 = f32[2048,2048,1]{1,0,2:T(8,128)S(1)} fusion(), kind=kLoop, calls=%fused_computation.9.clone.clone.clone.clone.1 | loop fusion | flops 197132288 | bytes 16777216 | tf_op jit(solution)/shard_map/ij,ajc->aic/dot_general | solution.py:35
  32.3 0.0 copy-done.2
  32.4 0.0 copy-done
  32.4 8.1 multiply_multiply_fusion
  40.5 143.1 %fusion.21 = f32[8,2048,128]{1,2,0:T(8,128)} fusion(f32[8,2048,128]{2,1,0:T(8,128)} %bitcast.34, f32[2048,2048,1]{1,0,2:T(8,128)S(1)} %fusion.63), kind=kOutput, calls=%fused_computation.33 | convolution fusion | flops 51539607552 | bytes 33554432 | tf_op jit(solution)/shard_map/ij,ajc->aic/dot_general | solution.py:35
  183.6 9.3 copy.21
  192.9 10.2 fusion.32
  203.1 4.7 copy.22
  207.8 1.4 collective-permute-start
  209.2 13.1 collective-permute-done
  222.3 9.8 add_select_fusion.7
  232.1 1.4 collective-permute-start.1
  233.5 180.6 %collective-permute-done.1 = f32[16384,128]{1,0:T(8,128)} collective-permute-done((f32[16384,128]{1,0:T(8,128)}, f32[16384,128]{1,0:T(8,128)}, u32[]{:S(2)}, u32[]{:S(2)}) %collective-permute-start.1) | collective-permute-done | bytes 8388640 | tf_op jit(solution)/shard_map/ppermute | solution.py:17
  414.1 9.8 add_select_fusion.6
  423.9 3.0 collective-permute-start.2
  426.8 179.6 %collective-permute-done.2 = f32[16384,128]{1,0:T(8,128)} collective-permute-done((f32[16384,128]{1,0:T(8,128)}, f32[16384,128]{1,0:T(8,128)}, u32[]{:S(2)}, u32[]{:S(2)}) %collective-permute-start.2) | collective-permute-done | bytes 8388640 | tf_op jit(solution)/shard_map/ppermute | solution.py:17
  606.5 9.8 add_select_fusion.5
  616.2 1.2 collective-permute-start.3
  617.5 178.9 %collective-permute-done.3 = f32[16384,128]{1,0:T(8,128)} collective-permute-done((f32[16384,128]{1,0:T(8,128)}, f32[16384,128]{1,0:T(8,128)}, u32[]{:S(2)}, u32[]{:S(2)}) %collective-permute-start.3) | collective-permute-done | bytes 8388640 | tf_op jit(solution)/shard_map/ppermute | solution.py:17
  796.4 9.8 add_select_fusion.4
  806.2 2.8 collective-permute-start.4
  808.9 178.0 %collective-permute-done.4 = f32[16384,128]{1,0:T(8,128)} collective-permute-done((f32[16384,128]{1,0:T(8,128)}, f32[16384,128]{1,0:T(8,128)}, u32[]{:S(2)}, u32[]{:S(2)}) %collective-permute-start.4) | collective-permute-done | bytes 8388640 | tf_op jit(solution)/shard_map/ppermute | solution.py:17
  986.9 9.8 add_select_fusion.3
  996.7 1.6 collective-permute-start.5
  998.3 0.0 copy-start.3
  998.3 177.0 %collective-permute-done.5 = f32[16384,128]{1,0:T(8,128)} collective-permute-done((f32[16384,128]{1,0:T(8,128)}, f32[16384,128]{1,0:T(8,128)}, u32[]{:S(2)}, u32[]{:S(2)}) %collective-permute-start.5) | collective-permute-done | bytes 8388640 | tf_op jit(solution)/shard_map/ppermute | solution.py:17
  1175.3 9.8 add_select_fusion.2
  1185.1 3.2 collective-permute-start.6
  1188.3 0.0 copy-done.3
  1188.4 0.8 all_to_all.9
  1189.1 12.5 all-to-all-start
  1201.6 169.1 %all-to-all-done = s32[128,1,2]{2,1,0:T(1,128)S(1)} async-done(((s32[128,1,2]{2,1,0:T(1,128)}), s32[128,1,2]{2,1,0:T(1,128)S(1)}, u32[]{:S(2)}, u32[]{:S(2)}) %all-to-all-start) | async-done | bytes 1056 | tf_op jit(solution)/shard_map/all_to_all | solution.py:56
  1370.7 0.5 broadcast.134
  1371.2 0.8 reduce.9
  1372.0 0.1 reshape.80
  1372.2 0.0 collective-permute-done.6
  1372.2 9.8 add_select_fusion.1
  1382.0 4.1 gather_fusion
  1386.1 0.9 broadcast_select_fusion
  1386.9 9.4 all-to-all-start.1
  1396.4 0.0 all-reduce.2.cloned.1.call-start
  1396.5 9.9 all-to-all-done.1
  1406.4 1.2 scatter_custom_fusion
  1407.6 0.0 copy-start.1
  1407.6 0.4 fusion.55
  1408.0 1.1 broadcast_multiply_fusion.1
  1409.1 0.0 all-reduce.2.cloned.1.call-update
  1409.2 143.3 %all-reduce.2.cloned.1.call-done = f32[16,128,128]{1,2,0:T(8,128)} async-done(((f32[16,128,128]{1,2,0:T(8,128)}), f32[16,128,128]{1,2,0:T(8,128)}) %all-reduce.2.cloned.1.call-update) | async-done | bytes 1048592 | tf_op jit(solution)/shard_map/psum | solution.py:71
  1552.5 1.3 broadcast_multiply_fusion
  1553.8 0.3 copy.24
  1554.1 1.4 fusion.24
  1555.5 187.5 %custom-call.4 = f32[16,128,128]{2,1,0:T(8,128)S(1)} custom-call(f32[16,128,128]{2,1,0:T(8,128)S(1)} %fusion.24), custom_call_target="Cholesky" | custom-call | tf_op jit(solution)/shard_map/jit(cholesky)/cholesky | solution.py:72
  1743.0 0.1 select_reduce_fusion
  1743.1 0.1 compare_reduce_fusion
  1743.3 0.2 select_bitcast_fusion
  1743.4 1.3 copy.25
  1744.7 0.0 copy-done.1
  (9 shorter events, 0.1 us)
Async XLA Ops:
  7.2 25.2 %copy-start.2 = (s32[16384]{0:T(1024)S(1)}, s32[16384]{0:T(1024)}, u32[]{:S(2)}) copy-start(s32[16384]{0:T(1024)} %param.4) | copy-start | bytes 196612
  7.2 25.2 %copy-start = (f32[16384,128]{1,0:T(8,128)S(1)}, f32[16384,128]{1,0:T(8,128)}, u32[]{:S(2)}) copy-start(f32[16384,128]{1,0:T(8,128)} %param.3) | copy-start | bytes 25165828
  207.8 14.6 collective-permute-start
  232.1 182.0 %collective-permute-start.1 = (f32[16384,128]{1,0:T(8,128)}, f32[16384,128]{1,0:T(8,128)}, u32[]{:S(2)}, u32[]{:S(2)}) collective-permute-start(f32[16384,128]{1,0:T(8,128)} %add_select_fusion.7), channel_id=1, source_target_pairs={{0,2},{1,3},{2,0},{3,1},{4,6},{5,7},{6,4},{7,5},{8,10},{9,11},{10,... | collective-permute-start | bytes 25165832 | tf_op jit(solution)/shard_map/ppermute | solution.py:17
  423.9 182.6 %collective-permute-start.2 = (f32[16384,128]{1,0:T(8,128)}, f32[16384,128]{1,0:T(8,128)}, u32[]{:S(2)}, u32[]{:S(2)}) collective-permute-start(f32[16384,128]{1,0:T(8,128)} %add_select_fusion.6), channel_id=1, source_target_pairs={{0,4},{1,5},{2,6},{3,7},{4,0},{5,1},{6,2},{7,3},{8,12},{9,13},{10,... | collective-permute-start | bytes 25165832 | tf_op jit(solution)/shard_map/ppermute | solution.py:17
  616.2 180.2 %collective-permute-start.3 = (f32[16384,128]{1,0:T(8,128)}, f32[16384,128]{1,0:T(8,128)}, u32[]{:S(2)}, u32[]{:S(2)}) collective-permute-start(f32[16384,128]{1,0:T(8,128)} %add_select_fusion.5), channel_id=1, source_target_pairs={{0,8},{1,9},{2,10},{3,11},{4,12},{5,13},{6,14},{7,15},{8,0},{9,1},... | collective-permute-start | bytes 25165832 | tf_op jit(solution)/shard_map/ppermute | solution.py:17
  806.2 180.7 %collective-permute-start.4 = (f32[16384,128]{1,0:T(8,128)}, f32[16384,128]{1,0:T(8,128)}, u32[]{:S(2)}, u32[]{:S(2)}) collective-permute-start(f32[16384,128]{1,0:T(8,128)} %add_select_fusion.4), channel_id=1, source_target_pairs={{0,16},{1,17},{2,18},{3,19},{4,20},{5,21},{6,22},{7,23},{8,24},{9,... | collective-permute-start | bytes 25165832 | tf_op jit(solution)/shard_map/ppermute | solution.py:17
  996.7 178.6 %collective-permute-start.5 = (f32[16384,128]{1,0:T(8,128)}, f32[16384,128]{1,0:T(8,128)}, u32[]{:S(2)}, u32[]{:S(2)}) collective-permute-start(f32[16384,128]{1,0:T(8,128)} %add_select_fusion.3), channel_id=1, source_target_pairs={{0,32},{1,33},{2,34},{3,35},{4,36},{5,37},{6,38},{7,39},{8,40},{9,... | collective-permute-start | bytes 25165832 | tf_op jit(solution)/shard_map/ppermute | solution.py:17
  998.3 190.0 %copy-start.3 = (s32[256]{0:T(256)S(1)}, s32[256]{0:T(256)}, u32[]{:S(2)}) copy-start(s32[256]{0:T(256)} %param.5) | copy-start | bytes 3076
  1185.1 187.1 %collective-permute-start.6 = (f32[16384,128]{1,0:T(8,128)}, f32[16384,128]{1,0:T(8,128)}, u32[]{:S(2)}, u32[]{:S(2)}) collective-permute-start(f32[16384,128]{1,0:T(8,128)} %add_select_fusion.2), channel_id=1, source_target_pairs={{0,64},{1,65},{2,66},{3,67},{4,68},{5,69},{6,70},{7,71},{8,72},{9,... | collective-permute-start | bytes 25165832 | tf_op jit(solution)/shard_map/ppermute | solution.py:17
  1189.1 181.5 %all-to-all-start = ((s32[128,1,2]{2,1,0:T(1,128)}), s32[128,1,2]{2,1,0:T(1,128)S(1)}, u32[]{:S(2)}, u32[]{:S(2)}) async-start(s32[128,1,2]{2,1,0:T(1,128)} %bitcast), calls=%async_computation | async-start | bytes 131072 | tf_op jit(solution)/shard_map/all_to_all | solution.py:56
  1386.9 19.5 %all-to-all-start.1 = ((f32[128,2,128]{2,1,0:T(2,128)}), f32[128,2,128]{2,1,0:T(2,128)S(1)}, u32[]{:S(2)}, u32[]{:S(2)}) async-start(f32[128,2,128]{2,1,0:T(2,128)} %broadcast_select_fusion), calls=%async_computation.1 | async-start | bytes 262144 | tf_op jit(solution)/shard_map/all_to_all | solution.py:60
  1396.4 156.1 %all-reduce.2.cloned.1.call-start = ((), (), s32[]{:S(2)}) async-start(), calls=%async_computation.2 | async-start | bytes 2097152 | tf_op jit(solution)/shard_map/psum | solution.py:71
  1407.6 337.1 %copy-start.1 = (f32[256,128]{1,0:T(8,128)}, f32[256,128]{1,0:T(8,128)S(1)}, u32[]{:S(2)}) copy-start(f32[256,128]{1,0:T(8,128)S(1)} %scatter_custom_fusion) | copy-start | bytes 393220
Sparse Core Ops, SparseCore 0:
  1409.3 143.1 all-reduce.1
where the time goes:
time: 1760 us; the launch traced here: 1750 us
  waiting for transfers between devices  1230 us (70%)
  other arithmetic  295 us (17%)
  matrix products  154 us (9%)
  starting transfers between devices  36.6 us (2%)
  local copies, waits for them, and re-layouts  22.4 us (1%)
    ppermute x7, waiting for transfers between devices, swapped(): return lax.ppermute(value, axis, pairs)  907 us
    another operation x4, other arithmetic, body(): lower = jnp.linalg.cholesky(grams / SAMP_OWN)  188 us
    all_to_all x1, waiting for transfers between devices, body(): lax.all_to_all(wanted, 'rows', split_axis=0, concat_axis=0, tiled=True)  169 us
    psum x1, waiting for transfers between devices, body(): grams = lax.psum(slot_mask * partial_gram[None], 'rows')  143 us
    dot_general x1, matrix products, local_transform(): jnp.einsum('ij,ajc->aic', sylvester(inner), blocks, precision=highest)  143 us
    select_n x7, other arithmetic, body(): source = jnp.where(upper, partner - source, source + partner)  68.4 us
  transfers between devices with their start and end apart: 10, of which 9 were waited for; matrix products, arithmetic and copies ran while one was open for 0% of the time, Pallas kernels for 0%

commit v1 on v0

v1 whole, which is shorter than its diff:
```python
import functools
import math

import jax
import jax.numpy as jnp
from jax import lax
from jax.experimental import pallas as pl
from jax.experimental.pallas import tpu as pltpu
from jax.sharding import PartitionSpec as P

MESH = pl.DeviceIdType.MESH
F32 = jnp.float32
BF16 = jnp.bfloat16
I32 = jnp.int32

TICKS = 8
STREAMS = 4
ROWS = 2097152
SAMP_OWN = 2048


def dot_tt(lhs, rhs, precision=None):
    return lax.dot_general(
        lhs, rhs, (((0,), (0,)), ((), ())), precision=precision, preferred_element_type=F32
    )


def iota(shape, dim):
    return lax.broadcasted_iota(I32, shape, dim)


def odd(bits):
    bits = bits ^ (bits >> 4)
    bits = bits ^ (bits >> 2)
    bits = bits ^ (bits >> 1)
    return bits & 1


def split2(value):
    high = value.astype(BF16)
    return high, (value - high.astype(F32)).astype(BF16)


def split3(value):
    high = value.astype(BF16)
    rest = value - high.astype(F32)
    mid = rest.astype(BF16)
    return high, mid, (rest - mid.astype(F32)).astype(BF16)


def kernel(
    matrix_ref, signs_ref, samples_ref, sketch_ref, factors_ref,
    X, SIB, P1, R1, R2, R3, R4, T3, R5, Y8, IDX, ML, SO, SS, POS, WF, WALL, G, RG1, RG2, GF, U, OUT,
    load_sem, y_send, y_recv, x_send, x_recv, z_send, z_recv, sib_send, sib_recv,
    s1, r1, s2, r2, s3, r3, s4, r4, s5, r5,
    w_send, w_recv, g1_send, g1_recv, g2_send, g2_recv, g3_send, g3_recv,
    ax_send, ax_recv, az_send, az_recv, ay_send, ay_recv, ac_send, ac_recv, out_sem,
):
    me = lax.axis_index("rows")
    core = me % 2
    y_pos = (me // 2) % 4
    x_pos = (me // 8) % 4
    z_pos = me // 32
    sibling = me + 1 - 2 * core

    def along(stride, hop):
        pos = (me // stride) % 4
        return me + ((pos + hop) % 4 - pos) * stride

    def axis_of(order, stage):
        k = (order + stage) % 3
        stride = 32 - 33 * k + 9 * k * k
        return stride, (me // stride) % 4

    def send(src, dst, send_sem, recv_sem, device):
        copy = pltpu.make_async_remote_copy(
            src_ref=src, dst_ref=dst, send_sem=send_sem, recv_sem=recv_sem,
            device_id=(device,), device_id_type=MESH,
        )
        copy.start()

    def wait(ref, sem):
        pltpu.make_async_copy(ref, ref, sem).wait()

    def load(chunk):
        return pltpu.make_async_copy(matrix_ref.at[chunk], X.at[chunk], load_sem.at[chunk])

    for chunk in range(16):
        load(chunk).start()

    group = [(dy, dc) for dy in range(4) for dc in range(2) if (dy, dc) != (0, 0)]

    def mate(dy, dc):
        return along(2, dy) + dc * (1 - 2 * core)

    barrier = pltpu.get_barrier_semaphore()
    for dy, dc in group:
        pl.semaphore_signal(barrier, inc=1, device_id=(mate(dy, dc),), device_id_type=MESH)
    for hop in (1, 2, 3):
        pl.semaphore_signal(barrier, inc=1, device_id=(along(8, hop),), device_id_type=MESH)
        pl.semaphore_signal(barrier, inc=1, device_id=(along(32, hop),), device_id_type=MESH)

    samples = samples_ref[...]
    part = (samples >> 7) & 127
    intervals = jnp.concatenate([part[0:1], part[1:2]], axis=1)
    values = jnp.concatenate([samples[0:1], samples[1:2]], axis=1)
    onehot = iota((128, 256), 0) == intervals
    onehot_f = jnp.where(onehot, 1.0, 0.0)
    before = jnp.where(iota((256, 256), 0) < iota((256, 256), 1), 1.0, 0.0).astype(BF16)
    count = jnp.dot(onehot_f.astype(BF16), before, preferred_element_type=F32)
    rank = jnp.sum(count * onehot_f, axis=0, keepdims=True).astype(I32)
    place = (
        (intervals >> 6) * 128 + (intervals & 7) * 16 + ((intervals >> 3) & 7) * 2 + rank
    )
    POS[...] = place
    slot = rank * 128 + intervals
    chosen = jnp.where(iota((256, 256), 0) == slot, 1.0, 0.0).astype(BF16)
    row8 = iota((8, 256), 0)
    fields = jnp.where(row8 == 0, values & 127, jnp.where(row8 == 1, values >> 14, 0))
    sorted_fields = lax.dot_general(
        fields.astype(F32).astype(BF16), chosen, (((1,), (1,)), ((), ())), preferred_element_type=F32
    ).astype(I32)
    sorted_rows = (
        sorted_fields[1:2] * 16384 + (iota((1, 256), 1) & 127) * 128 + sorted_fields[0:1]
    )
    mine8 = 2 * y_pos + core
    Y8[mine8, 0:1, :] = sorted_rows[:, :128]
    Y8[mine8, 1:2, :] = sorted_rows[:, 128:]
    pl.semaphore_wait(barrier, 13)
    for n, (dy, dc) in enumerate(group):
        send(Y8.at[mine8], Y8.at[mine8], y_send.at[n], y_recv.at[n], mate(dy, dc))

    had = (1 - 2 * odd(iota((128, 128), 0) & iota((128, 128), 1))).astype(F32)

    def front(chunk, carry):
        load(chunk).wait()
        for al in range(8):
            high, low = split2(X[chunk, al])
            sign = signs_ref[pl.ds(chunk * 8 + al, 1), :].astype(F32)
            signed = (had * sign).astype(BF16)
            X[chunk, al] = jnp.dot(
                jnp.concatenate([signed, signed], axis=1),
                jnp.concatenate([high, low], axis=0),
                preferred_element_type=F32,
            )
        for tile in range(16):
            rows = slice(8 * tile, 8 * tile + 8)
            v = [X[chunk, al, rows, :] for al in range(8)]
            for span in (1, 2, 4):
                v = butterfly(v, span)
            for al in range(8):
                X[chunk, al, rows, :] = v[al]
        return carry

    def butterfly(v, span):
        out = list(v)
        for n in range(len(v)):
            if n & span == 0:
                out[n] = v[n] + v[n + span]
                out[n + span] = v[n] - v[n + span]
        return out

    lax.fori_loop(0, 5, front, 0)
    for n in range(7):
        wait(Y8.at[0], y_recv.at[n])
    for q in range(8):
        for j in range(2):
            IDX[z_pos, x_pos, j, q : q + 1, :] = Y8[q, j : j + 1, :]
    for hop in (1, 2, 3):
        block = IDX.at[z_pos, x_pos]
        send(block, block, x_send.at[hop - 1], x_recv.at[hop - 1], along(8, hop))
    lax.fori_loop(5, 10, front, 0)
    for hop in (1, 2, 3):
        wait(IDX.at[0, 0], x_recv.at[hop - 1])
    for hop in (1, 2, 3):
        block = IDX.at[z_pos]
        send(block, block, z_send.at[hop - 1], z_recv.at[hop - 1], along(32, hop))
    lax.fori_loop(10, 16, front, 0)

    def second(step):
        def tile_step(tile, carry):
            rows = pl.ds(pl.multiple_of(tile * 8, 8), 8)
            v = [X[ah, step, rows, :] for ah in range(16)]
            for span in (1, 2, 4, 8):
                v = butterfly(v, span)
            for ah in range(16):
                X[ah, step, rows, :] = v[ah]
            return carry

        lax.fori_loop(0, 16, tile_step, 0)
        send(
            X.at[pl.ds((1 - core) * 8, 8), step], SIB.at[step], sib_send.at[step], sib_recv.at[step], sibling
        )

    second(0)

    for hop in (1, 2, 3):
        wait(IDX.at[0], z_recv.at[hop - 1])
    from_t = iota((128, 128), 0)
    to_t = iota((128, 128), 1)
    hi_t, mid_t, lo_t, core_t = to_t // 32, (to_t // 8) % 4, (to_t // 2) % 4, to_t % 2
    natural = [
        hi_t * 32 + mid_t * 8 + lo_t * 2 + core_t,
        hi_t * 8 + mid_t * 2 + lo_t * 32 + core_t,
        hi_t * 2 + mid_t * 32 + lo_t * 8 + core_t,
    ]
    for order in range(3):
        perm = jnp.where(from_t == natural[order], 1.0, 0.0).astype(BF16)
        for j in range(2):
            rows = IDX[:, :, j].reshape(128, 128)
            low = (rows & 127).astype(F32).astype(BF16)
            block = (rows >> 14).astype(F32).astype(BF16)
            ML[order, j] = dot_tt(low, perm).astype(I32)
            owner = dot_tt(block, perm).astype(I32)
            SO[order, j] = (1 - 2 * odd(owner & me)).astype(F32)
            SS[order, j] = (1 - 2 * odd(owner & sibling)).astype(F32)

    sub = iota((128, 128), 0)

    def order_of(s, tick):
        return s if s < 3 else tick % 3

    def produce(tick):
        def one(n, carry):
            s = n // 2
            order = s + (s // 3) * (tick % 3 - 3)
            p = (core * 8 + n) * 8 + tick
            own_hi, own_lo = split2(X[core * 8 + n, tick])
            sib_hi, sib_lo = split2(SIB[tick, n])
            picks = []
            for j in range(2):
                hit = sub == ML[order, j, pl.ds(p, 1), :]
                own = jnp.where(hit, SO[order, j, pl.ds(p, 1), :], 0.0).astype(BF16)
                sib = jnp.where(hit, SS[order, j, pl.ds(p, 1), :], 0.0).astype(BF16)
                picks.append(jnp.concatenate([own, sib], axis=0))
            pick = jnp.concatenate(picks, axis=1)
            got = dot_tt(pick, jnp.concatenate([own_hi, sib_hi], axis=0))
            got = got + dot_tt(pick, jnp.concatenate([own_lo, sib_lo], axis=0))
            P1[tick, s, n % 2] = got.reshape(2, 4, 4, 8, 128)
            return carry

        lax.fori_loop(0, 8, one, 0)

    def first_send(tick):
        for s in range(STREAMS):
            stride, a = axis_of(order_of(s, tick), 0)
            far = (a + 2) % 4
            send(P1.at[tick, s, :, 0, far], R1.at[tick, s, 0], s1.at[tick], r1.at[tick], along(stride, 1))
            send(P1.at[tick, s, :, 1, far], R1.at[tick, s, 1], s1.at[tick], r1.at[tick], along(stride, 3))

    def first_pass(tick):
        wait(R1.at[tick], r1.at[tick])
        for s in range(STREAMS):
            stride, a = axis_of(order_of(s, tick), 0)
            up, down = (a + 1) % 4, (a + 3) % 4
            P1[tick, s, :, 0, up] += R1[tick, s, 0]
            P1[tick, s, :, 1, down] += R1[tick, s, 1]
            send(P1.at[tick, s, :, :, up], R2.at[tick, s, 0], s2.at[tick], r2.at[tick], along(stride, 1))
            send(P1.at[tick, s, :, :, down], R2.at[tick, s, 1], s2.at[tick], r2.at[tick], along(stride, 3))

    def second_send(tick):
        wait(R2.at[tick], r2.at[tick])
        for s in range(STREAMS):
            _, a = axis_of(order_of(s, tick), 0)
            P1[tick, s, :, :, a] += R2[tick, s, 0] + R2[tick, s, 1]
            stride, b = axis_of(order_of(s, tick), 1)
            far = (b + 2) % 4
            send(P1.at[tick, s, :, 0, a, far], R3.at[tick, s, 0], s3.at[tick], r3.at[tick], along(stride, 1))
            send(P1.at[tick, s, :, 1, a, far], R3.at[tick, s, 1], s3.at[tick], r3.at[tick], along(stride, 3))

    def second_pass(tick):
        wait(R3.at[tick], r3.at[tick])
        for s in range(STREAMS):
            _, a = axis_of(order_of(s, tick), 0)
            stride, b = axis_of(order_of(s, tick), 1)
            up, down = (b + 1) % 4, (b + 3) % 4
            P1[tick, s, :, 0, a, up] += R3[tick, s, 0]
            P1[tick, s, :, 1, a, down] += R3[tick, s, 1]
            send(P1.at[tick, s, :, :, a, up], R4.at[tick, s, 0], s4.at[tick], r4.at[tick], along(stride, 1))
            send(P1.at[tick, s, :, :, a, down], R4.at[tick, s, 1], s4.at[tick], r4.at[tick], along(stride, 3))

    def third_send(tick):
        wait(R4.at[tick], r4.at[tick])
        for s in range(STREAMS):
            _, a = axis_of(order_of(s, tick), 0)
            _, b = axis_of(order_of(s, tick), 1)
            total = P1[tick, s, :, :, a, b] + R4[tick, s, 0] + R4[tick, s, 1]
            for g in range(2):
                for j in range(2):
                    for q in range(4):
                        for ct in range(2):
                            row = ct * 4 + g * 2 + j
                            T3[tick, s, q, row : row + 1, :] = total[g, j, 2 * q + ct : 2 * q + ct + 1, :]
            stride, d = axis_of(order_of(s, tick), 2)
            for hop in (1, 2, 3):
                send(
                    T3.at[tick, s, (d + hop) % 4], R5.at[tick, s, hop - 1], s5.at[tick], r5.at[tick],
                    along(stride, hop),
                )

    scale = 1.0 / math.sqrt(ROWS)

    def last(tick):
        wait(R5.at[tick], r5.at[tick])
        done = []
        for s in range(STREAMS):
            _, d = axis_of(order_of(s, tick), 2)
            done.append((T3[tick, s, d] + R5[tick, s, 0] + R5[tick, s, 1] + R5[tick, s, 2]) * scale)
        for ct in range(2):
            for pair in range(2):
                rows = pl.ds(pl.multiple_of(tick * 16 + pair * 8, 8), 8)
                WF[ct, rows, :] = jnp.concatenate(
                    [done[2 * pair][4 * ct : 4 * ct + 4], done[2 * pair + 1][4 * ct : 4 * ct + 4]], axis=0
                )

    def tick_step(i, carry):
        @pl.when(i + 1 < TICKS)
        def _():
            second(i + 1)

        @pl.when(i < TICKS)
        def _():
            wait(SIB.at[i], sib_recv.at[i])
            produce(i)
            first_send(i)

        for lag, work in enumerate((first_pass, second_send, second_pass, third_send, last), 1):

            @pl.when((i >= lag) & (i < TICKS + lag))
            def _():
                work(i - lag)

        return carry

    lax.fori_loop(0, TICKS + 5, tick_step, 0)

    send(WF.at[1 - core], WALL.at[core], w_send, w_recv, sibling)
    mine = WF[...].reshape(256, 128)
    gram = dot_tt(mine, mine, lax.Precision.HIGHEST) * (1.0 / SAMP_OWN)
    G[...] = gram.reshape(2, 4, 16, 128)
    send(G.at[1 - core], RG1, g1_send, g1_recv, sibling)
    wait(RG1, g1_recv)
    wait(G.at[0], g1_send)
    G[core] += RG1[...]
    for hop in (1, 2, 3):
        send(G.at[core, (y_pos + hop) % 4], RG2.at[hop - 1], g2_send.at[hop - 1], g2_recv.at[hop - 1], along(2, hop))
    for hop in (1, 2, 3):
        wait(RG2.at[0], g2_recv.at[hop - 1])
    GF[core, y_pos] = G[core, y_pos] + RG2[0] + RG2[1] + RG2[2]
    block = GF.at[core, y_pos]
    for n, (dy, dc) in enumerate(group):
        send(block, block, g3_send.at[n], g3_recv.at[n], mate(dy, dc))
    for n in range(7):
        wait(GF.at[0, 0], g3_recv.at[n])

    sub8 = iota((8, 128), 0)
    lane8 = iota((8, 128), 1)
    work = GF[...].reshape(128, 128)
    for kb in range(16):
        panel = work[:8]
        for j in range(8):
            col = panel[:, 8 * kb + j : 8 * kb + j + 1]
            inv = lax.rsqrt(col[j : j + 1])
            row = panel[j : j + 1] * inv
            panel = jnp.where(sub8 > j, panel - (col * inv) * row, jnp.where(sub8 == j, row, panel))
        panel = jnp.where(lane8 >= 8 * kb + sub8, panel, 0.0)
        U[8 * kb : 8 * kb + 8, :] = panel
        if kb < 15:
            update = dot_tt(panel, panel, lax.Precision.HIGHEST)
            work = work[8:] - update[8 * kb + 8 :]

    OUT[z_pos, x_pos, core, y_pos] = U[pl.ds(pl.multiple_of(core * 64 + y_pos * 16, 16), 16), :]
    block = OUT.at[z_pos, x_pos, core, y_pos]
    for hop in (1, 2, 3):
        send(block, block, ax_send.at[hop - 1], ax_recv.at[hop - 1], along(8, hop))

    WALL[core] = WF[core]
    wait(WALL.at[0], w_recv)
    back = jnp.where(iota((256, 256), 0) == POS[...], 1.0, 0.0).astype(BF16)
    sketch_ref[...] = sum(dot_tt(back, term) for term in split3(WALL[...].reshape(256, 128)))

    for hop in (1, 2, 3):
        wait(OUT.at[0, 0, 0, 0], ax_recv.at[hop - 1])
    block = OUT.at[z_pos, :, core, y_pos]
    for hop in (1, 2, 3):
        send(block, block, az_send.at[hop - 1], az_recv.at[hop - 1], along(32, hop))
    for hop in (1, 2, 3):
        wait(OUT.at[0, :, 0, 0], az_recv.at[hop - 1])
    block = OUT.at[:, :, core, y_pos]
    for hop in (1, 2, 3):
        send(block, block, ay_send.at[hop - 1], ay_recv.at[hop - 1], along(2, hop))
    for hop in (1, 2, 3):
        wait(OUT.at[:, :, 0, 0], ay_recv.at[hop - 1])
    block = OUT.at[:, :, core]
    send(block, block, ac_send, ac_recv, sibling)
    wait(OUT.at[:, :, 0], ac_recv)
    final = pltpu.make_async_copy(OUT, factors_ref, out_sem)
    final.start()

    for n in range(7):
        wait(Y8.at[0], y_send.at[n])
        wait(GF.at[0, 0], g3_send.at[n])
    for n in range(3):
        wait(IDX.at[0, 0], x_send.at[n])
        wait(IDX.at[0], z_send.at[n])
        wait(RG2.at[0], g2_send.at[n])
        wait(OUT.at[0, 0, 0, 0], ax_send.at[n])
        wait(OUT.at[0, :, 0, 0], az_send.at[n])
        wait(OUT.at[:, :, 0, 0], ay_send.at[n])
    wait(OUT.at[:, :, 0], ac_send)
    wait(WALL.at[0], w_send)

    def sent(tick, carry):
        wait(SIB.at[tick], sib_send.at[tick])
        wait(R1.at[tick], s1.at[tick])
        wait(R2.at[tick], s2.at[tick])
        wait(R3.at[tick], s3.at[tick])
        wait(R4.at[tick], s4.at[tick])
        wait(R5.at[tick], s5.at[tick])
        return carry

    lax.fori_loop(0, TICKS, sent, 0)
    final.wait()


def body(matrix, signs, samples):
    dma = pltpu.SemaphoreType.DMA
    vmem = pltpu.VMEM
    t, s = TICKS, STREAMS
    sketch, factors = pl.pallas_call(
        kernel,
        out_shape=(
            jax.ShapeDtypeStruct((256, 128), F32),
            jax.ShapeDtypeStruct((4, 4, 2, 4, 16, 128), F32),
        ),
        in_specs=[
            pl.BlockSpec(memory_space=pl.ANY),
            pl.BlockSpec(memory_space=pltpu.VMEM),
            pl.BlockSpec(memory_space=pltpu.VMEM),
        ],
        out_specs=(pl.BlockSpec(memory_space=pltpu.VMEM), pl.BlockSpec(memory_space=pl.ANY)),
        scratch_shapes=[
            vmem((16, 8, 128, 128), F32),
            vmem((8, 8, 128, 128), F32),
            vmem((t, s, 2, 2, 4, 4, 8, 128), F32),
            vmem((t, s, 2, 2, 4, 8, 128), F32),
            vmem((t, s, 2, 2, 2, 4, 8, 128), F32),
            vmem((t, s, 2, 2, 8, 128), F32),
            vmem((t, s, 2, 2, 2, 8, 128), F32),
            vmem((t, s, 4, 8, 128), F32),
            vmem((t, s, 3, 8, 128), F32),
            vmem((8, 8, 128), I32),
            vmem((4, 4, 2, 8, 128), I32),
            vmem((3, 2, 128, 128), I32),
            vmem((3, 2, 128, 128), F32),
            vmem((3, 2, 128, 128), F32),
            vmem((1, 256), I32),
            vmem((2, 128, 128), F32),
            vmem((2, 128, 128), F32),
            vmem((2, 4, 16, 128), F32),
            vmem((4, 16, 128), F32),
            vmem((3, 16, 128), F32),
            vmem((2, 4, 16, 128), F32),
            vmem((128, 128), F32),
            vmem((4, 4, 2, 4, 16, 128), F32),
            dma((16,)), dma((7,)), dma((7,)), dma((3,)), dma((3,)), dma((3,)), dma((3,)),
            dma((t,)), dma((t,)),
            dma((t,)), dma((t,)), dma((t,)), dma((t,)), dma((t,)), dma((t,)), dma((t,)), dma((t,)),
            dma((t,)), dma((t,)),
            dma(()), dma(()), dma(()), dma(()), dma((3,)), dma((3,)), dma((7,)), dma((7,)),
            dma((3,)), dma((3,)), dma((3,)), dma((3,)), dma((3,)), dma((3,)), dma(()), dma(()), dma(()),
        ],
        compiler_params=pltpu.CompilerParams(
            collective_id=0, has_side_effects=True, vmem_limit_bytes=48 * 1024 * 1024
        ),
    )(matrix.reshape(16, 8, 128, 128), signs.reshape(128, 128), samples.reshape(2, 128))
    return sketch, factors.reshape(16, 128, 128)


def solution(mesh):
    return jax.shard_map(
        body,
        mesh=mesh,
        in_specs=(P("rows", None), P("rows"), P("rows")),
        out_specs=(P("rows", None), P()),
        check_vma=False,
    )
```

time: 1760 us -> 116 us (0.07)
  waiting for transfers between devices: 1230 us -> 0 us
  other arithmetic: 295 us -> 0 us
  matrix products: 154 us -> 0 us
  Pallas kernels: 0 us -> 112 us
  starting transfers between devices: 36.6 us -> 0 us
  local copies, waits for them, and re-layouts: 22.4 us -> 3.14 us
    ppermute x7 -> x0, waiting for transfers between devices: 907 us -> none  [swapped(): return lax.ppermute(value, axis, pairs)]
    another operation x4 -> x0, other arithmetic: 188 us -> none  [body(): lower = jnp.linalg.cholesky(grams / SAMP_OWN)]
    all_to_all x2 -> x0, waiting for transfers between devices: 179 us -> none  [the longest x1 169 us: body(): lax.all_to_all(wanted, 'rows', split_axis=0, concat_axis=0, tiled=True)]
    dot_general x3 -> x0, matrix products: 154 us -> none  [the longest x1 143 us: local_transform(): jnp.einsum('ij,ajc->aic', sylvester(inner), blocks, precision=highest)]
    psum x1 -> x0, waiting for transfers between devices: 143 us -> none  [body(): grams = lax.psum(slot_mask * partial_gram[None], 'rows')]
    pallas_call x0 -> x1, Pallas kernels: none -> 112 us  [body(): pl.pallas_call(kernel, out_shape=(jax.ShapeDtypeStruct((256, 128), F32),...]
    select_n x10 -> x0, other arithmetic: 69.3 us -> none  [the longest x7 68.4 us: body(): source = jnp.where(upper, partner - source, source + partner)]
    dot_general x1 -> x0, other arithmetic: 25.2 us -> none  [local_transform(): jnp.einsum('ij,ajc->aic', sylvester(inner), blocks, precision=highest)]
  transfers between devices with their start and end apart: 10 -> 0, of which waited for: 9 -> 0; matrix products, arithmetic and copies ran while one was open for 0% -> 0% of each run, Pallas kernels for 0% -> 0%
where the time goes in v1:
time: 116 us; the launch traced here: 115 us
  Pallas kernels  112 us (97%)
  local copies, waits for them, and re-layouts  3.14 us (3%)
    pallas_call x1, Pallas kernels, body(): pl.pallas_call(kernel, out_shape=(jax.ShapeDtypeStruct((256, 128), F32),...  112 us
    unnamed x6, local copies, waits for them, and re-layouts  3.14 us

profile of v1, /device:TPU:1, one launch (start us, length us, event | category | flops | bytes accessed | tf_op | source)
XLA Modules:
  0.0 115.5 jit_solution(13167623349286821866)
XLA Ops:
  0.6 0.0 copy-start
  0.6 0.8 copy-done
  1.5 0.0 copy-start.1
  1.5 0.7 copy-done.1
  2.1 111.7 %shard_map.50 = (f32[256,128]{1,0:T(8,128)S(1)}, f32[4,4,2,4,16,128]{5,4,3,2,1,0:T(8,128)S(1)}) custom-call(f32[16,8,128,128]{3,2,1,0:T(8,128)} %bitcast.7, s32[128,128]{1,0:T(8,128)S(1)} %bitcast.5, s32[2,128]{1,0:T(2,128)S(1)} %bitcast.6), custom_call_target="tpu_custom_call" | custom-call | tf_op jit(solution)/shard_map/pallas_call | solution.py:430
  113.9 0.7 copy.7
  114.5 1.0 copy.8
Async XLA Ops:
  0.6 0.8 copy-start
  1.5 0.7 copy-start.1

commit v2 on v1

v2 whole, which is shorter than its diff:
```python
import functools
import math

import jax
import jax.numpy as jnp
from jax import lax
from jax.experimental import pallas as pl
from jax.experimental.pallas import tpu as pltpu
from jax.sharding import PartitionSpec as P

MESH = pl.DeviceIdType.MESH
F32 = jnp.float32
BF16 = jnp.bfloat16
I32 = jnp.int32

TICKS = 8
LAG = 2
DIRECT = 2
STREAMS = 4
ROWS = 2097152
SAMP_OWN = 2048


def dot_tt(lhs, rhs, precision=None):
    return lax.dot_general(
        lhs, rhs, (((0,), (0,)), ((), ())), precision=precision, preferred_element_type=F32
    )


def iota(shape, dim):
    return lax.broadcasted_iota(I32, shape, dim)


def odd(bits):
    bits = bits ^ (bits >> 4)
    bits = bits ^ (bits >> 2)
    bits = bits ^ (bits >> 1)
    return bits & 1


def split2(value):
    high = value.astype(BF16)
    return high, (value - high.astype(F32)).astype(BF16)


def split3(value):
    high = value.astype(BF16)
    rest = value - high.astype(F32)
    mid = rest.astype(BF16)
    return high, mid, (rest - mid.astype(F32)).astype(BF16)


def kernel(
    matrix_ref, signs_ref, samples_ref, sketch_ref, factors_ref,
    X, SIB, P1, R1, R2, R3, R4, T3, R5, Y8, IDX, SGN, SMP, ML, SO, SS, POS, WF, WALL, G, RG1, RG2, GF, OUT, DUM,
    load_sem, in_sem, y_send, y_recv, p_send, p_recv, sib_send, sib_recv,
    s1, r1, s2, r2, s3, r3, s4, r4, s5, r5,
    w_send, w_recv, g1_send, g1_recv, g2_send, g2_recv, g3_send, g3_recv,
    o_send, o_recv, f_send, f_recv, out_sem,
):
    me = lax.axis_index("rows")
    core = me % 2
    y_pos = (me // 2) % 4
    x_pos = (me // 8) % 4
    z_pos = me // 32
    sibling = me + 1 - 2 * core

    def along(stride, hop):
        pos = (me // stride) % 4
        return me + ((pos + hop) % 4 - pos) * stride

    def axis_of(order, stage):
        k = (order + stage) % 3
        stride = 32 - 33 * k + 9 * k * k
        return stride, (me // stride) % 4

    def send(src, dst, send_sem, recv_sem, device):
        copy = pltpu.make_async_remote_copy(
            src_ref=src, dst_ref=dst, send_sem=send_sem, recv_sem=recv_sem,
            device_id=(device,), device_id_type=MESH,
        )
        copy.start()

    def wait(ref, sem):
        pltpu.make_async_copy(ref, ref, sem).wait()

    def load(chunk):
        return pltpu.make_async_copy(matrix_ref.at[chunk], X.at[chunk], load_sem.at[chunk])

    fetch_samples = pltpu.make_async_copy(samples_ref, SMP, in_sem.at[0])
    fetch_samples.start()
    fetch_signs = pltpu.make_async_copy(signs_ref, SGN, in_sem.at[1])
    fetch_signs.start()
    for chunk in range(16):
        load(chunk).start()

    group = [(dy, dc) for dy in range(4) for dc in range(2) if (dy, dc) != (0, 0)]
    plane = [(dz, dx) for dz in range(4) for dx in range(4) if (dz, dx) != (0, 0)]

    def mate(dy, dc):
        return along(2, dy) + dc * (1 - 2 * core)

    def peer(dz, dx):
        return ((z_pos + dz) % 4) * 32 + ((x_pos + dx) % 4) * 8 + me % 8

    barrier = pltpu.get_barrier_semaphore()
    for dy, dc in group:
        pl.semaphore_signal(barrier, inc=1, device_id=(mate(dy, dc),), device_id_type=MESH)
    for dz, dx in plane:
        pl.semaphore_signal(barrier, inc=1, device_id=(peer(dz, dx),), device_id_type=MESH)

    had = (1 - 2 * odd(iota((128, 128), 0) & iota((128, 128), 1))).astype(F32)
    fetch_samples.wait()

    samples = SMP[...]
    part = (samples >> 7) & 127
    intervals = jnp.concatenate([part[0:1], part[1:2]], axis=1)
    values = jnp.concatenate([samples[0:1], samples[1:2]], axis=1)
    onehot = iota((128, 256), 0) == intervals
    onehot_f = jnp.where(onehot, 1.0, 0.0)
    before = jnp.where(iota((256, 256), 0) < iota((256, 256), 1), 1.0, 0.0).astype(BF16)
    count = jnp.dot(onehot_f.astype(BF16), before, preferred_element_type=F32)
    rank = jnp.sum(count * onehot_f, axis=0, keepdims=True).astype(I32)
    place = (
        (intervals >> 6) * 128 + (intervals & 7) * 16 + ((intervals >> 3) & 7) * 2 + rank
    )
    POS[...] = place
    slot = rank * 128 + intervals
    chosen = jnp.where(iota((256, 256), 0) == slot, 1.0, 0.0).astype(BF16)
    row8 = iota((8, 256), 0)
    fields = jnp.where(row8 == 0, values & 127, jnp.where(row8 == 1, values >> 14, 0))
    sorted_fields = lax.dot_general(
        fields.astype(F32).astype(BF16), chosen, (((1,), (1,)), ((), ())), preferred_element_type=F32
    ).astype(I32)
    sorted_rows = (
        sorted_fields[1:2] * 16384 + (iota((1, 256), 1) & 127) * 128 + sorted_fields[0:1]
    )
    mine8 = 2 * y_pos + core
    Y8[mine8, 0:1, :] = sorted_rows[:, :128]
    Y8[mine8, 1:2, :] = sorted_rows[:, 128:]
    def front(chunk, carry):
        load(chunk).wait()
        for al in range(8):
            high, low = split2(X[chunk, al])
            sign = SGN[pl.ds(chunk * 8 + al, 1), :].astype(F32)
            signed = (had * sign).astype(BF16)
            X[chunk, al] = jnp.dot(
                jnp.concatenate([signed, signed], axis=1),
                jnp.concatenate([high, low], axis=0),
                preferred_element_type=F32,
            )
        for tile in range(16):
            rows = slice(8 * tile, 8 * tile + 8)
            v = [X[chunk, al, rows, :] for al in range(8)]
            for span in (1, 2, 4):
                v = butterfly(v, span)
            for al in range(8):
                X[chunk, al, rows, :] = v[al]
        return carry

    def butterfly(v, span):
        out = list(v)
        for n in range(len(v)):
            if n & span == 0:
                out[n] = v[n] + v[n + span]
                out[n + span] = v[n] - v[n + span]
        return out

    fetch_signs.wait()
    lax.fori_loop(0, 3, front, 0)
    pl.semaphore_wait(barrier, 22)
    for n, (dy, dc) in enumerate(group):
        send(Y8.at[mine8], Y8.at[mine8], y_send.at[n], y_recv.at[n], mate(dy, dc))
    lax.fori_loop(3, 10, front, 0)
    for n in range(7):
        wait(Y8.at[0], y_recv.at[n])
    for q in range(8):
        for j in range(2):
            IDX[z_pos, x_pos, j, q : q + 1, :] = Y8[q, j : j + 1, :]
    for dz, dx in plane:
        send(IDX.at[z_pos, x_pos], IDX.at[z_pos, x_pos], p_send, p_recv, peer(dz, dx))
    lax.fori_loop(10, 16, front, 0)

    def second(step):
        def tile_step(tile, carry):
            rows = pl.ds(pl.multiple_of(tile * 8, 8), 8)
            v = [X[ah, step, rows, :] for ah in range(16)]
            for span in (1, 2, 4, 8):
                v = butterfly(v, span)
            for ah in range(16):
                X[ah, step, rows, :] = v[ah]
            return carry

        lax.fori_loop(0, 16, tile_step, 0)
        send(
            X.at[pl.ds((1 - core) * 8, 8), step], SIB.at[step], sib_send.at[step], sib_recv.at[step], sibling
        )

    for step in range(TICKS):
        second(step)

    wait(DUM, p_recv)
    from_t = iota((128, 128), 0)
    to_t = iota((128, 128), 1)
    hi_t, mid_t, lo_t, core_t = to_t // 32, (to_t // 8) % 4, (to_t // 2) % 4, to_t % 2
    natural = [
        hi_t * 32 + mid_t * 8 + lo_t * 2 + core_t,
        hi_t * 8 + mid_t * 2 + lo_t * 32 + core_t,
        hi_t * 2 + mid_t * 32 + lo_t * 8 + core_t,
    ]
    for order in range(3):
        perm = jnp.where(from_t == natural[order], 1.0, 0.0).astype(BF16)
        for j in range(2):
            rows = IDX[:, :, j].reshape(128, 128)
            low = (rows & 127).astype(F32).astype(BF16)
            block = (rows >> 14).astype(F32).astype(BF16)
            ML[order, j] = dot_tt(low, perm).astype(I32)
            owner = dot_tt(block, perm).astype(I32)
            SO[order, j] = (1 - 2 * odd(owner & me)).astype(F32)
            SS[order, j] = (1 - 2 * odd(owner & sibling)).astype(F32)

    sub = iota((128, 128), 0)

    def order_of(s, tick):
        return s if s < 3 else tick % 3

    def produce(tick):
        def one(n, carry):
            s = n // 2
            order = s + (s // 3) * (tick % 3 - 3)
            p = (core * 8 + n) * 8 + tick
            own_hi, own_lo = split2(X[core * 8 + n, tick])
            sib_hi, sib_lo = split2(SIB[tick, n])
            picks = []
            for j in range(2):
                hit = sub == ML[order, j, pl.ds(p, 1), :]
                own = jnp.where(hit, SO[order, j, pl.ds(p, 1), :], 0.0).astype(BF16)
                sib = jnp.where(hit, SS[order, j, pl.ds(p, 1), :], 0.0).astype(BF16)
                picks.append(jnp.concatenate([own, sib], axis=0))
            pick = jnp.concatenate(picks, axis=1)
            terms = jnp.concatenate(
                [jnp.concatenate([own_hi, sib_hi], axis=0), jnp.concatenate([own_lo, sib_lo], axis=0)], axis=1
            )
            got = dot_tt(pick, terms)
            got = got[:, :128] + got[:, 128:]
            P1[tick, s, n % 2] = got.reshape(2, 4, 4, 8, 128)
            return carry

        lax.fori_loop(0, 8, one, 0, unroll=2)

    def spread(tick, s, slabs, near, far, sems, stride, pos):
        over = (pos + 2) % 4
        (near_send, near_recv), (far_send, far_recv) = sems

        @pl.when(tick < TICKS - DIRECT)
        def _():
            for half, hop in ((0, 1), (1, 3)):
                send(slabs(over).at[:, half], far.at[tick, s, :, half], far_send, far_recv, along(stride, hop))

        @pl.when(tick >= TICKS - DIRECT)
        def _():
            send(slabs(over), far.at[tick, s], far_send, far_recv, along(stride, 2))
            for slot, hop in ((0, 1), (1, 3)):
                send(slabs((pos + hop) % 4), near.at[tick, s, slot], near_send, near_recv, along(stride, hop))

    def relay(tick, s, slabs, near, far, sems, stride, pos):
        near_send, near_recv = sems
        for slot, hop in ((0, 1), (1, 3)):
            slab = slabs((pos + hop) % 4)
            slab[:, slot] += far[tick, s, :, slot]
            send(slab, near.at[tick, s, slot], near_send, near_recv, along(stride, hop))

    def slabs_of(tick, s):
        return lambda q: P1.at[tick, s, :, :, q]

    def parts_of(tick, s, a):
        return lambda q: P1.at[tick, s, :, :, a, q]

    def first_send(tick):
        sems = ((s2.at[tick], r2.at[tick]), (s1.at[tick], r1.at[tick]))
        for s in range(STREAMS):
            spread(tick, s, slabs_of(tick, s), R2, R1, sems, *axis_of(order_of(s, tick), 0))

    def first_pass(tick):
        wait(R1.at[tick], r1.at[tick])

        @pl.when(tick < TICKS - DIRECT)
        def _():
            for s in range(STREAMS):
                sems = (s2.at[tick], r2.at[tick])
                relay(tick, s, slabs_of(tick, s), R2, R1, sems, *axis_of(order_of(s, tick), 0))

    def second_send(tick):
        wait(R2.at[tick], r2.at[tick])
        sems = ((s4.at[tick], r4.at[tick]), (s3.at[tick], r3.at[tick]))
        for s in range(STREAMS):
            _, a = axis_of(order_of(s, tick), 0)
            P1[tick, s, :, :, a] += R2[tick, s, 0] + R2[tick, s, 1]

            @pl.when(tick >= TICKS - DIRECT)
            def _():
                P1[tick, s, :, :, a] += R1[tick, s]

            spread(tick, s, parts_of(tick, s, a), R4, R3, sems, *axis_of(order_of(s, tick), 1))

    def second_pass(tick):
        wait(R3.at[tick], r3.at[tick])

        @pl.when(tick < TICKS - DIRECT)
        def _():
            for s in range(STREAMS):
                _, a = axis_of(order_of(s, tick), 0)
                sems = (s4.at[tick], r4.at[tick])
                relay(tick, s, parts_of(tick, s, a), R4, R3, sems, *axis_of(order_of(s, tick), 1))

    def third_send(tick):
        wait(R4.at[tick], r4.at[tick])
        for s in range(STREAMS):
            _, a = axis_of(order_of(s, tick), 0)
            _, b = axis_of(order_of(s, tick), 1)

            @pl.when(tick >= TICKS - DIRECT)
            def _():
                P1[tick, s, :, :, a, b] += R3[tick, s]

            total = P1[tick, s, :, :, a, b] + R4[tick, s, 0] + R4[tick, s, 1]
            for g in range(2):
                for j in range(2):
                    for q in range(4):
                        for ct in range(2):
                            row = ct * 4 + g * 2 + j
                            T3[tick, s, q, row : row + 1, :] = total[g, j, 2 * q + ct : 2 * q + ct + 1, :]
            stride, d = axis_of(order_of(s, tick), 2)
            for hop in (1, 2, 3):
                send(
                    T3.at[tick, s, (d + hop) % 4], R5.at[tick, s, hop - 1], s5.at[tick], r5.at[tick],
                    along(stride, hop),
                )

    scale = 1.0 / math.sqrt(ROWS)

    def last(tick):
        wait(R5.at[tick], r5.at[tick])
        done = []
        for s in range(STREAMS):
            _, d = axis_of(order_of(s, tick), 2)
            done.append((T3[tick, s, d] + R5[tick, s, 0] + R5[tick, s, 1] + R5[tick, s, 2]) * scale)
        for ct in range(2):
            for pair in range(2):
                rows = pl.ds(pl.multiple_of(tick * 16 + pair * 8, 8), 8)
                WF[ct, rows, :] = jnp.concatenate(
                    [done[2 * pair][4 * ct : 4 * ct + 4], done[2 * pair + 1][4 * ct : 4 * ct + 4]], axis=0
                )

    def tick_step(i, carry):
        @pl.when(i < TICKS)
        def _():
            wait(SIB.at[i], sib_recv.at[i])
            produce(i)
            first_send(i)

        for n, work in enumerate((first_pass, second_send, second_pass, third_send, last), 1):
            lag = n * LAG

            @pl.when((i >= lag) & (i < TICKS + lag))
            def _():
                work(i - lag)

        return carry

    lax.fori_loop(0, TICKS + 5 * LAG, tick_step, 0)

    send(WF.at[1 - core], WALL.at[core], w_send, w_recv, sibling)
    high, mid, low = split3(WF[...].reshape(256, 128))
    square = dot_tt(high, jnp.concatenate([high, mid], axis=1))
    rest = dot_tt(mid, jnp.concatenate([mid, low], axis=1))
    outer = dot_tt(high, low)
    cross = square[:, 128:] + outer
    gram = square[:, :128] + rest[:, :128] + (cross + cross.T)
    G[...] = (gram * (1.0 / SAMP_OWN)).reshape(2, 64, 128)
    send(G.at[1 - core], RG1, g1_send, g1_recv, sibling)
    wait(RG1, g1_recv)
    G[core] += RG1[...]
    for hop in (1, 2, 3):
        send(G.at[core], RG2.at[hop - 1], g2_send.at[hop - 1], g2_recv.at[hop - 1], along(2, hop))

    WALL[core] = WF[core]
    wait(WALL.at[0], w_recv)
    back = jnp.where(iota((256, 256), 0) == POS[...], 1.0, 0.0).astype(BF16)
    sketch_ref[...] = sum(dot_tt(back, term) for term in split3(WALL[...].reshape(256, 128)))

    for hop in (1, 2, 3):
        wait(RG2.at[0], g2_recv.at[hop - 1])
    terms = [G[core], RG2[0], RG2[1], RG2[2]]
    GF[core] = (terms[0] + terms[2]) + (terms[1] + terms[3])
    send(GF.at[core], GF.at[core], g3_send, g3_recv, sibling)
    wait(GF.at[0], g3_recv)

    sub16 = iota((16, 128), 0)
    lane16 = iota((16, 128), 1)
    work = GF[...].reshape(128, 128)
    for r in range(8):
        panel = work[:16]
        columns = [jnp.broadcast_to(panel[:, 16 * r + k : 16 * r + k + 1], (16, 128)) for k in range(16)]
        scales = jnp.zeros((16, 128), F32)
        for j in range(16):
            inverse = lax.rsqrt(columns[j][j : j + 1])
            square = inverse * inverse
            below = jnp.where(sub16 > j, columns[j], 0.0)
            scales = jnp.where(sub16 == j, inverse, scales)
            for k in range(j + 1, 16):
                columns[k] = columns[k] - (below * columns[k][j : j + 1]) * square
            panel = panel - (below * panel[j : j + 1]) * square
        panel = jnp.where(lane16 >= 16 * r + sub16, panel * scales, 0.0)

        @pl.when(core == r % 2)
        def _():
            OUT[z_pos, x_pos, r] = panel
            block = OUT.at[z_pos, x_pos, r]
            for dz, dx in plane:
                send(block, block, o_send.at[r // 2], o_recv.at[r // 2], peer(dz, dx))

        if r < 7:
            h, m, l = (term.astype(F32) for term in split3(panel))
            lhs = jnp.concatenate([h, h, m, m, h, l], axis=0).astype(BF16)
            rhs = jnp.concatenate([h, m, h, m, l, h], axis=0).astype(BF16)
            work = work[16:] - dot_tt(lhs, rhs)[16 * r + 16 :]

    def share(n):
        slab = OUT.at[:, :, 2 * n + core]
        wait(DUM, o_recv.at[n])
        send(slab, slab, f_send.at[n], f_recv.at[n], sibling)
        return pltpu.make_async_copy(slab, factors_ref.at[:, :, 2 * n + core], out_sem.at[n])

    def store(n):
        return pltpu.make_async_copy(
            OUT.at[:, :, 2 * n + 1 - core], factors_ref.at[:, :, 2 * n + 1 - core], out_sem.at[4 + n]
        )

    for n in range(4):
        share(n).start()
    for n in range(4):
        wait(OUT.at[:, :, 0], f_recv.at[n])
        store(n).start()

    for n in range(7):
        wait(Y8.at[0], y_send.at[n])
    wait(DUM, p_send)
    for n in range(3):
        wait(RG2.at[0], g2_send.at[n])
    for n in range(4):
        wait(DUM, o_send.at[n])
        wait(OUT.at[:, :, 0], f_send.at[n])
    wait(GF.at[0], g3_send)
    wait(RG1, g1_send)
    wait(WALL.at[0], w_send)

    def sent(tick, carry):
        wait(SIB.at[tick], sib_send.at[tick])
        wait(R1.at[tick], s1.at[tick])
        wait(R2.at[tick], s2.at[tick])
        wait(R3.at[tick], s3.at[tick])
        wait(R4.at[tick], s4.at[tick])
        wait(R5.at[tick], s5.at[tick])
        return carry

    lax.fori_loop(0, TICKS, sent, 0)
    for n in range(8):
        wait(OUT.at[:, :, 0], out_sem.at[n])


def body(matrix, signs, samples):
    dma = pltpu.SemaphoreType.DMA
    vmem = pltpu.VMEM
    t, s = TICKS, STREAMS
    sketch, factors = pl.pallas_call(
        kernel,
        out_shape=(
            jax.ShapeDtypeStruct((256, 128), F32),
            jax.ShapeDtypeStruct((4, 4, 8, 16, 128), F32),
        ),
        in_specs=[pl.BlockSpec(memory_space=pl.ANY)] * 3,
        out_specs=(pl.BlockSpec(memory_space=pltpu.VMEM), pl.BlockSpec(memory_space=pl.ANY)),
        scratch_shapes=[
            vmem((16, 8, 128, 128), F32),
            vmem((8, 8, 128, 128), F32),
            vmem((t, s, 2, 2, 4, 4, 8, 128), F32),
            vmem((t, s, 2, 2, 4, 8, 128), F32),
            vmem((t, s, 2, 2, 2, 4, 8, 128), F32),
            vmem((t, s, 2, 2, 8, 128), F32),
            vmem((t, s, 2, 2, 2, 8, 128), F32),
            vmem((t, s, 4, 8, 128), F32),
            vmem((t, s, 3, 8, 128), F32),
            vmem((8, 8, 128), I32),
            vmem((4, 4, 2, 8, 128), I32),
            vmem((128, 128), I32),
            vmem((2, 128), I32),
            vmem((3, 2, 128, 128), I32),
            vmem((3, 2, 128, 128), F32),
            vmem((3, 2, 128, 128), F32),
            vmem((1, 256), I32),
            vmem((2, 128, 128), F32),
            vmem((2, 128, 128), F32),
            vmem((2, 64, 128), F32),
            vmem((64, 128), F32),
            vmem((3, 64, 128), F32),
            vmem((2, 64, 128), F32),
            vmem((4, 4, 8, 16, 128), F32),
            vmem((15, 16, 128), F32),
            dma((16,)), dma((2,)), dma((7,)), dma((7,)), dma(()), dma(()),
            dma((t,)), dma((t,)),
            dma((t,)), dma((t,)), dma((t,)), dma((t,)), dma((t,)), dma((t,)), dma((t,)), dma((t,)),
            dma((t,)), dma((t,)),
            dma(()), dma(()), dma(()), dma(()), dma((3,)), dma((3,)), dma(()), dma(()),
            dma((4,)), dma((4,)), dma((4,)), dma((4,)), dma((8,)),
        ],
        compiler_params=pltpu.CompilerParams(
            collective_id=0, has_side_effects=True, vmem_limit_bytes=48 * 1024 * 1024
        ),
    )(matrix.reshape(16, 8, 128, 128), signs.reshape(128, 128), samples.reshape(2, 128))
    return sketch, factors.reshape(16, 128, 128)


def solution(mesh):
    return jax.shard_map(
        body,
        mesh=mesh,
        in_specs=(P("rows", None), P("rows"), P("rows")),
        out_specs=(P("rows", None), P()),
        check_vma=False,
    )
```

time: 116 us -> 84.7 us (0.73)
  Pallas kernels: 112 us -> 80.7 us
    pallas_call x1, Pallas kernels: 112 us -> 80.7 us  [body(): pl.pallas_call(kernel, out_shape=(jax.ShapeDtypeStruct((256, 128), F32),...]
where the time goes in v2:
time: 84.7 us; the launch traced here: 84.5 us
  Pallas kernels  80.7 us (95%)
  local copies, waits for them, and re-layouts  3.14 us (4%)
    pallas_call x1, Pallas kernels, body(): pl.pallas_call(kernel, out_shape=(jax.ShapeDtypeStruct((256, 128), F32),...  80.7 us
    unnamed x6, local copies, waits for them, and re-layouts  3.14 us

profile of v2, /device:TPU:1, one launch (start us, length us, event | category | flops | bytes accessed | tf_op | source)
XLA Modules:
  0.0 84.5 jit_solution(5920718782381982414)
XLA Ops:
  0.6 0.0 copy-start
  0.6 0.8 copy-done
  1.5 0.0 copy-start.1
  1.5 0.7 copy-done.1
  2.1 80.7 %shard_map.50 = (f32[256,128]{1,0:T(8,128)S(1)}, f32[4,4,8,16,128]{4,3,2,1,0:T(8,128)S(1)}) custom-call(f32[16,8,128,128]{3,2,1,0:T(8,128)} %bitcast.7, s32[128,128]{1,0:T(8,128)S(1)} %bitcast.5, s32[2,128]{1,0:T(2,128)S(1)} %bitcast.6), custom_call_target="tpu_custom_call" | custom-call | tf_op jit(solution)/shard_map/pallas_call | solution.py:476
  82.9 0.7 copy.7
  83.5 1.0 %copy.8 = f32[16,128,128]{2,1,0:T(8,128)} copy(f32[16,128,128]{2,1,0:T(8,128)S(1)} %bitcast.4) | data formatting | bytes 2097152
Async XLA Ops:
  0.6 0.8 copy-start
  1.5 0.7 copy-start.1

commit v3 on v2

--- a/solution.py
+++ b/solution.py
@@ -14,8 +14,6 @@
 I32 = jnp.int32
 
 TICKS = 8
-LAG = 2
-DIRECT = 2
 STREAMS = 4
 ROWS = 2097152
 SAMP_OWN = 2048
@@ -167,11 +165,11 @@
         return out
 
     fetch_signs.wait()
-    lax.fori_loop(0, 3, front, 0)
+    lax.fori_loop(0, 4, front, 0, unroll=2)
     pl.semaphore_wait(barrier, 22)
     for n, (dy, dc) in enumerate(group):
         send(Y8.at[mine8], Y8.at[mine8], y_send.at[n], y_recv.at[n], mate(dy, dc))
-    lax.fori_loop(3, 10, front, 0)
+    lax.fori_loop(4, 10, front, 0, unroll=2)
     for n in range(7):
         wait(Y8.at[0], y_recv.at[n])
     for q in range(8):
@@ -179,7 +177,7 @@
             IDX[z_pos, x_pos, j, q : q + 1, :] = Y8[q, j : j + 1, :]
     for dz, dx in plane:
         send(IDX.at[z_pos, x_pos], IDX.at[z_pos, x_pos], p_send, p_recv, peer(dz, dx))
-    lax.fori_loop(10, 16, front, 0)
+    lax.fori_loop(10, 16, front, 0, unroll=2)
 
     def second(step):
         def tile_step(tile, carry):
@@ -191,7 +189,7 @@
                 X[ah, step, rows, :] = v[ah]
             return carry
 
-        lax.fori_loop(0, 16, tile_step, 0)
+        lax.fori_loop(0, 16, tile_step, 0, unroll=2)
         send(
             X.at[pl.ds((1 - core) * 8, 8), step], SIB.at[step], sib_send.at[step], sib_recv.at[step], sibling
         )
@@ -246,22 +244,12 @@
             P1[tick, s, n % 2] = got.reshape(2, 4, 4, 8, 128)
             return carry
 
-        lax.fori_loop(0, 8, one, 0, unroll=2)
-
-    def spread(tick, s, slabs, near, far, sems, stride, pos):
+        lax.fori_loop(0, 8, one, 0, unroll=8)
+
+    def spread(tick, s, slabs, far, sems, stride, pos):
         over = (pos + 2) % 4
-        (near_send, near_recv), (far_send, far_recv) = sems
-
-        @pl.when(tick < TICKS - DIRECT)
-        def _():
-            for half, hop in ((0, 1), (1, 3)):
-                send(slabs(over).at[:, half], far.at[tick, s, :, half], far_send, far_recv, along(stride, hop))
-
-        @pl.when(tick >= TICKS - DIRECT)
-        def _():
-            send(slabs(over), far.at[tick, s], far_send, far_recv, along(stride, 2))
-            for slot, hop in ((0, 1), (1, 3)):
-                send(slabs((pos + hop) % 4), near.at[tick, s, slot], near_send, near_recv, along(stride, hop))
+        for half, hop in ((0, 1), (1, 3)):
+            send(slabs(over).at[:, half], far.at[tick, s, :, half], *sems, along(stride, hop))
 
     def relay(tick, s, slabs, near, far, sems, stride, pos):
         near_send, near_recv = sems
@@ -277,52 +265,34 @@
         return lambda q: P1.at[tick, s, :, :, a, q]
 
     def first_send(tick):
-        sems = ((s2.at[tick], r2.at[tick]), (s1.at[tick], r1.at[tick]))
-        for s in range(STREAMS):
-            spread(tick, s, slabs_of(tick, s), R2, R1, sems, *axis_of(order_of(s, tick), 0))
+        for s in range(STREAMS):
+            spread(tick, s, slabs_of(tick, s), R1, (s1.at[tick], r1.at[tick]), *axis_of(order_of(s, tick), 0))
 
     def first_pass(tick):
         wait(R1.at[tick], r1.at[tick])
-
-        @pl.when(tick < TICKS - DIRECT)
-        def _():
-            for s in range(STREAMS):
-                sems = (s2.at[tick], r2.at[tick])
-                relay(tick, s, slabs_of(tick, s), R2, R1, sems, *axis_of(order_of(s, tick), 0))
+        for s in range(STREAMS):
+            sems = (s2.at[tick], r2.at[tick])
+            relay(tick, s, slabs_of(tick, s), R2, R1, sems, *axis_of(order_of(s, tick), 0))
 
     def second_send(tick):
         wait(R2.at[tick], r2.at[tick])
-        sems = ((s4.at[tick], r4.at[tick]), (s3.at[tick], r3.at[tick]))
         for s in range(STREAMS):
             _, a = axis_of(order_of(s, tick), 0)
             P1[tick, s, :, :, a] += R2[tick, s, 0] + R2[tick, s, 1]
-
-            @pl.when(tick >= TICKS - DIRECT)
-            def _():
-                P1[tick, s, :, :, a] += R1[tick, s]
-
-            spread(tick, s, parts_of(tick, s, a), R4, R3, sems, *axis_of(order_of(s, tick), 1))
+            spread(tick, s, parts_of(tick, s, a), R3, (s3.at[tick], r3.at[tick]), *axis_of(order_of(s, tick), 1))
 
     def second_pass(tick):
         wait(R3.at[tick], r3.at[tick])
-
-        @pl.when(tick < TICKS - DIRECT)
-        def _():
-            for s in range(STREAMS):
-                _, a = axis_of(order_of(s, tick), 0)
-                sems = (s4.at[tick], r4.at[tick])
-                relay(tick, s, parts_of(tick, s, a), R4, R3, sems, *axis_of(order_of(s, tick), 1))
+        for s in range(STREAMS):
+            _, a = axis_of(order_of(s, tick), 0)
+            sems = (s4.at[tick], r4.at[tick])
+            relay(tick, s, parts_of(tick, s, a), R4, R3, sems, *axis_of(order_of(s, tick), 1))
 
     def third_send(tick):
         wait(R4.at[tick], r4.at[tick])
         for s in range(STREAMS):
             _, a = axis_of(order_of(s, tick), 0)
             _, b = axis_of(order_of(s, tick), 1)
-
-            @pl.when(tick >= TICKS - DIRECT)
-            def _():
-                P1[tick, s, :, :, a, b] += R3[tick, s]
-
             total = P1[tick, s, :, :, a, b] + R4[tick, s, 0] + R4[tick, s, 1]
             for g in range(2):
                 for j in range(2):
@@ -352,23 +322,20 @@
                     [done[2 * pair][4 * ct : 4 * ct + 4], done[2 * pair + 1][4 * ct : 4 * ct + 4]], axis=0
                 )
 
-    def tick_step(i, carry):
-        @pl.when(i < TICKS)
-        def _():
-            wait(SIB.at[i], sib_recv.at[i])
-            produce(i)
-            first_send(i)
-
-        for n, work in enumerate((first_pass, second_send, second_pass, third_send, last), 1):
-            lag = n * LAG
-
-            @pl.when((i >= lag) & (i < TICKS + lag))
-            def _():
-                work(i - lag)
-
-        return carry
-
-    lax.fori_loop(0, TICKS + 5 * LAG, tick_step, 0)
+    def make(tick):
+        wait(SIB.at[tick], sib_recv.at[tick])
+        produce(tick)
+        first_send(tick)
+
+    def each(work):
+        def step(tick, carry):
+            work(tick)
+            return carry
+
+        lax.fori_loop(0, TICKS, step, 0)
+
+    for work in (make, first_pass, second_send, second_pass, third_send, last):
+        each(work)
 
     send(WF.at[1 - core], WALL.at[core], w_send, w_recv, sibling)
     high, mid, low = split3(WF[...].reshape(256, 128))
@@ -479,7 +446,7 @@
             jax.ShapeDtypeStruct((256, 128), F32),
             jax.ShapeDtypeStruct((4, 4, 8, 16, 128), F32),
         ),
-        in_specs=[pl.BlockSpec(memory_space=pl.ANY)] * 3,
+        in_specs=[pl.BlockSpec(memory_space=pltpu.HBM)] * 3,
         out_specs=(pl.BlockSpec(memory_space=pltpu.VMEM), pl.BlockSpec(memory_space=pl.ANY)),
         scratch_shapes=[
             vmem((16, 8, 128, 128), F32),

time: 84.7 us -> 77.7 us (0.917)
  Pallas kernels: 80.7 us -> 73.8 us
    pallas_call x1, Pallas kernels: 80.7 us -> 73.8 us  [body(): pl.pallas_call(kernel, out_shape=(jax.ShapeDtypeStruct((256, 128), F32),...]
where the time goes in v3:
time: 77.7 us; the launch traced here: 77.6 us
  Pallas kernels  73.8 us (95%)
  local copies, waits for them, and re-layouts  3.14 us (4%)
    pallas_call x1, Pallas kernels, body(): pl.pallas_call(kernel, out_shape=(jax.ShapeDtypeStruct((256, 128), F32),...  73.8 us
    unnamed x6, local copies, waits for them, and re-layouts  3.14 us

profile of v3, /device:TPU:1, one launch (start us, length us, event | category | flops | bytes accessed | tf_op | source)
XLA Modules:
  0.0 77.6 jit_solution(8190708539601957019)
XLA Ops:
  0.6 0.0 copy-start
  0.6 0.8 %copy-done = s32[16384]{0:T(1024)S(1)} copy-done((s32[16384]{0:T(1024)S(1)}, s32[16384]{0:T(1024)}, u32[]{:S(2)}) %copy-start) | copy-done | bytes 65560
  1.5 0.0 copy-start.1
  1.5 0.7 copy-done.1
  2.1 73.8 %shard_map.50 = (f32[256,128]{1,0:T(8,128)S(1)}, f32[4,4,8,16,128]{4,3,2,1,0:T(8,128)S(1)}) custom-call(f32[16,8,128,128]{3,2,1,0:T(8,128)} %bitcast.7, s32[128,128]{1,0:T(8,128)S(1)} %bitcast.5, s32[2,128]{1,0:T(2,128)S(1)} %bitcast.6), custom_call_target="tpu_custom_call" | custom-call | tf_op jit(solution)/shard_map/pallas_call | solution.py:443
  75.9 0.7 copy.7
  76.6 1.0 %copy.8 = f32[16,128,128]{2,1,0:T(8,128)} copy(f32[16,128,128]{2,1,0:T(8,128)S(1)} %bitcast.4) | data formatting | bytes 2097152
Async XLA Ops:
  0.6 0.8 %copy-start = (s32[16384]{0:T(1024)S(1)}, s32[16384]{0:T(1024)}, u32[]{:S(2)}) copy-start(s32[16384]{0:T(1024)} %param.4) | copy-start | bytes 196612
  1.5 0.7 copy-start.1

commit v4 on v3

--- a/solution.py
+++ b/solution.py
@@ -14,6 +14,7 @@
 I32 = jnp.int32
 
 TICKS = 8
+EARLY = 2
 STREAMS = 4
 ROWS = 2097152
 SAMP_OWN = 2048
@@ -50,9 +51,9 @@
 
 def kernel(
     matrix_ref, signs_ref, samples_ref, sketch_ref, factors_ref,
-    X, SIB, P1, R1, R2, R3, R4, T3, R5, Y8, IDX, SGN, SMP, ML, SO, SS, POS, WF, WALL, G, RG1, RG2, GF, OUT, DUM,
+    X, SIB, P1, R1, R2, R3, R4, T3, R5, Y8, IDX, SGN, SMP, ML, OW, EB, FT, ET, POS, WF, WALL, G, RG1, RG2, GF, OUT, DUM,
     load_sem, in_sem, y_send, y_recv, p_send, p_recv, sib_send, sib_recv,
-    s1, r1, s2, r2, s3, r3, s4, r4, s5, r5,
+    e_send, e_recv, x_send, x_recv, s1, r1, s2, r2, s3, r3, s4, r4, s5, r5,
     w_send, w_recv, g1_send, g1_recv, g2_send, g2_recv, g3_send, g3_recv,
     o_send, o_recv, f_send, f_recv, out_sem,
 ):
@@ -66,11 +67,6 @@
     def along(stride, hop):
         pos = (me // stride) % 4
         return me + ((pos + hop) % 4 - pos) * stride
-
-    def axis_of(order, stage):
-        k = (order + stage) % 3
-        stride = 32 - 33 * k + 9 * k * k
-        return stride, (me // stride) % 4
 
     def send(src, dst, send_sem, recv_sem, device):
         copy = pltpu.make_async_remote_copy(
@@ -194,7 +190,36 @@
             X.at[pl.ds((1 - core) * 8, 8), step], SIB.at[step], sib_send.at[step], sib_recv.at[step], sibling
         )
 
-    for step in range(TICKS):
+    def axis_of(order, stage):
+        k = (order + stage) % 3
+        stride = 32 - 33 * k + 9 * k * k
+        return stride, (me // stride) % 4
+
+    def block_of(s, q, sib):
+        return SIB.at[q // 2, 2 * s + q % 2] if sib else X.at[core * 8 + 2 * s + q % 2, q // 2]
+
+    def early_send(sib):
+        for s in range(3):
+            stride, a = axis_of(s, 0)
+            for hop in (1, 2, 3):
+                send(
+                    block_of(s, (a + hop) % 4, sib), EB.at[s, a, sib], e_send.at[s], e_recv.at[s],
+                    along(stride, hop),
+                )
+
+    second(0)
+    second(1)
+    early_send(0)
+    second(2)
+    second(3)
+    wait(SIB.at[0], sib_recv.at[0])
+    wait(SIB.at[1], sib_recv.at[1])
+    early_send(1)
+    for s in range(3):
+        _, a = axis_of(s, 0)
+        for sib in (0, 1):
+            EB[s, a, sib] = block_of(s, a, sib)[...]
+    for step in range(4, TICKS):
         second(step)
 
     wait(DUM, p_recv)
@@ -213,38 +238,52 @@
             low = (rows & 127).astype(F32).astype(BF16)
             block = (rows >> 14).astype(F32).astype(BF16)
             ML[order, j] = dot_tt(low, perm).astype(I32)
-            owner = dot_tt(block, perm).astype(I32)
-            SO[order, j] = (1 - 2 * odd(owner & me)).astype(F32)
-            SS[order, j] = (1 - 2 * odd(owner & sibling)).astype(F32)
+            OW[order, j] = dot_tt(block, perm).astype(I32)
 
     sub = iota((128, 128), 0)
 
     def order_of(s, tick):
         return s if s < 3 else tick % 3
 
-    def produce(tick):
+    def picked(order, p, device, own, sib):
+        picks = []
+        for j in range(2):
+            hit = sub == ML[order, j, pl.ds(p, 1), :]
+            owner = OW[order, j, pl.ds(p, 1), :]
+            for bits in (owner & device, owner & (device + 1 - 2 * core)):
+                picks.append(jnp.where(hit, (1 - 2 * odd(bits)).astype(F32), 0.0).astype(BF16))
+        pick = jnp.concatenate(
+            [jnp.concatenate(picks[:2], axis=0), jnp.concatenate(picks[2:], axis=0)], axis=1
+        )
+        own_hi, own_lo = split2(own)
+        sib_hi, sib_lo = split2(sib)
+        terms = jnp.concatenate(
+            [jnp.concatenate([own_hi, sib_hi], axis=0), jnp.concatenate([own_lo, sib_lo], axis=0)], axis=1
+        )
+        got = dot_tt(pick, terms)
+        return got[:, :128] + got[:, 128:]
+
+    def produce(tick, first):
         def one(n, carry):
             s = n // 2
             order = s + (s // 3) * (tick % 3 - 3)
             p = (core * 8 + n) * 8 + tick
-            own_hi, own_lo = split2(X[core * 8 + n, tick])
-            sib_hi, sib_lo = split2(SIB[tick, n])
-            picks = []
-            for j in range(2):
-                hit = sub == ML[order, j, pl.ds(p, 1), :]
-                own = jnp.where(hit, SO[order, j, pl.ds(p, 1), :], 0.0).astype(BF16)
-                sib = jnp.where(hit, SS[order, j, pl.ds(p, 1), :], 0.0).astype(BF16)
-                picks.append(jnp.concatenate([own, sib], axis=0))
-            pick = jnp.concatenate(picks, axis=1)
-            terms = jnp.concatenate(
-                [jnp.concatenate([own_hi, sib_hi], axis=0), jnp.concatenate([own_lo, sib_lo], axis=0)], axis=1
-            )
-            got = dot_tt(pick, terms)
-            got = got[:, :128] + got[:, 128:]
+            got = picked(order, p, me, X[core * 8 + n, tick], SIB[tick, n])
             P1[tick, s, n % 2] = got.reshape(2, 4, 4, 8, 128)
             return carry
 
-        lax.fori_loop(0, 8, one, 0, unroll=8)
+        lax.fori_loop(first, 8, one, 0, unroll=8 - first)
+
+    def produce_early(s, carry):
+        stride, a = axis_of(s, 0)
+        p = (core * 8 + 2 * s + a % 2) * 8 + a // 2
+        wait(EB.at[0, pl.ds(0, 3)], e_recv.at[s])
+        got = sum(picked(s, p, me + (q - a) * stride, EB[s, q, 0], EB[s, q, 1]) for q in range(4))
+        got = got.reshape(2, 4, 4, 8, 128)
+        for q in range(4):
+            for j in range(2):
+                P1[q // 2, s, q % 2, j, a] = got[j, q]
+        return carry
 
     def spread(tick, s, slabs, far, sems, stride, pos):
         over = (pos + 2) % 4
@@ -264,31 +303,35 @@
     def parts_of(tick, s, a):
         return lambda q: P1.at[tick, s, :, :, a, q]
 
-    def first_send(tick):
-        for s in range(STREAMS):
+    def wait_streams(ref, sem, tick, streams):
+        wait(ref.at[tick] if len(streams) == STREAMS else ref.at[tick, 3], sem.at[tick])
+
+    def first_send(tick, streams):
+        for s in streams:
             spread(tick, s, slabs_of(tick, s), R1, (s1.at[tick], r1.at[tick]), *axis_of(order_of(s, tick), 0))
 
-    def first_pass(tick):
-        wait(R1.at[tick], r1.at[tick])
-        for s in range(STREAMS):
+    def first_pass(tick, streams):
+        wait_streams(R1, r1, tick, streams)
+        for s in streams:
             sems = (s2.at[tick], r2.at[tick])
             relay(tick, s, slabs_of(tick, s), R2, R1, sems, *axis_of(order_of(s, tick), 0))
 
-    def second_send(tick):
-        wait(R2.at[tick], r2.at[tick])
+    def second_send(tick, streams):
+        wait_streams(R2, r2, tick, streams)
         for s in range(STREAMS):
             _, a = axis_of(order_of(s, tick), 0)
-            P1[tick, s, :, :, a] += R2[tick, s, 0] + R2[tick, s, 1]
+            if s in streams:
+                P1[tick, s, :, :, a] += R2[tick, s, 0] + R2[tick, s, 1]
             spread(tick, s, parts_of(tick, s, a), R3, (s3.at[tick], r3.at[tick]), *axis_of(order_of(s, tick), 1))
 
-    def second_pass(tick):
+    def second_pass(tick, streams):
         wait(R3.at[tick], r3.at[tick])
         for s in range(STREAMS):
             _, a = axis_of(order_of(s, tick), 0)
             sems = (s4.at[tick], r4.at[tick])
             relay(tick, s, parts_of(tick, s, a), R4, R3, sems, *axis_of(order_of(s, tick), 1))
 
-    def third_send(tick):
+    def third_send(tick, streams):
         wait(R4.at[tick], r4.at[tick])
         for s in range(STREAMS):
             _, a = axis_of(order_of(s, tick), 0)
@@ -309,12 +352,20 @@
 
     scale = 1.0 / math.sqrt(ROWS)
 
-    def last(tick):
+    def last(tick, streams):
         wait(R5.at[tick], r5.at[tick])
         done = []
         for s in range(STREAMS):
             _, d = axis_of(order_of(s, tick), 2)
             done.append((T3[tick, s, d] + R5[tick, s, 0] + R5[tick, s, 1] + R5[tick, s, 2]) * scale)
+            if s not in streams:
+                FT[tick, s] = done[s]
+        if len(streams) < STREAMS:
+            for ct in range(2):
+                WF[ct, pl.ds(pl.multiple_of(tick * 16 + 8, 8), 8), :] = jnp.concatenate(
+                    [done[3][4 * ct : 4 * ct + 4]] * 2, axis=0
+                )
+            return
         for ct in range(2):
             for pair in range(2):
                 rows = pl.ds(pl.multiple_of(tick * 16 + pair * 8, 8), 8)
@@ -322,20 +373,46 @@
                     [done[2 * pair][4 * ct : 4 * ct + 4], done[2 * pair + 1][4 * ct : 4 * ct + 4]], axis=0
                 )
 
-    def make(tick):
-        wait(SIB.at[tick], sib_recv.at[tick])
-        produce(tick)
-        first_send(tick)
-
-    def each(work):
+    def make(tick, streams):
+        if len(streams) == STREAMS:
+            wait(SIB.at[tick], sib_recv.at[tick])
+        produce(tick, 2 * streams[0])
+        first_send(tick, streams)
+
+    everything, late = (0, 1, 2, 3), (3,)
+
+    def each(work, start, stop, streams):
         def step(tick, carry):
-            work(tick)
+            work(tick, streams)
             return carry
 
-        lax.fori_loop(0, TICKS, step, 0)
+        lax.fori_loop(start, stop, step, 0)
 
     for work in (make, first_pass, second_send, second_pass, third_send, last):
-        each(work)
+        each(work, 0, EARLY, late)
+        if work is last:
+            for s in range(3):
+                stride, a = axis_of(s, 0)
+                for hop in (1, 2, 3):
+                    send(FT.at[((a + hop) % 4) // 2, s], ET.at[s, a], x_send.at[s], x_recv.at[s], along(stride, hop))
+                ET[s, a] = FT[a // 2, s]
+        each(work, EARLY, TICKS, everything)
+        if work is make:
+            lax.fori_loop(0, 3, produce_early, 0)
+
+    for s in range(3):
+        wait(ET.at[0, pl.ds(0, 3)], x_recv.at[s])
+    for tick in range(EARLY):
+        for ct in range(2):
+            rows = []
+            for s in range(3):
+                _, a = axis_of(s, 0)
+                for g in range(2):
+                    tile = ET[s, 2 * tick + g]
+                    pair = [tile[4 * ct + 2 * n : 4 * ct + 2 * n + 2] for n in range(2)]
+                    rows.append(jnp.where(a % 2 == 0, pair[0], pair[1]))
+            rows.append(WF[ct, 16 * tick + 12 : 16 * tick + 16, :])
+            WF[ct, 16 * tick : 16 * tick + 16, :] = jnp.concatenate(rows, axis=0)
 
     send(WF.at[1 - core], WALL.at[core], w_send, w_recv, sibling)
     high, mid, low = split3(WF[...].reshape(256, 128))
@@ -422,16 +499,20 @@
     wait(RG1, g1_send)
     wait(WALL.at[0], w_send)
 
-    def sent(tick, carry):
+    for s in range(3):
+        wait(EB.at[0, pl.ds(0, 3)], e_send.at[s])
+        wait(ET.at[0, pl.ds(0, 3)], x_send.at[s])
+
+    def sent(tick, streams):
         wait(SIB.at[tick], sib_send.at[tick])
-        wait(R1.at[tick], s1.at[tick])
-        wait(R2.at[tick], s2.at[tick])
+        wait_streams(R1, s1, tick, streams)
+        wait_streams(R2, s2, tick, streams)
         wait(R3.at[tick], s3.at[tick])
         wait(R4.at[tick], s4.at[tick])
         wait(R5.at[tick], s5.at[tick])
-        return carry
-
-    lax.fori_loop(0, TICKS, sent, 0)
+
+    each(sent, 0, EARLY, late)
+    each(sent, EARLY, TICKS, everything)
     for n in range(8):
         wait(OUT.at[:, :, 0], out_sem.at[n])
 
@@ -463,8 +544,10 @@
             vmem((128, 128), I32),
             vmem((2, 128), I32),
             vmem((3, 2, 128, 128), I32),
-            vmem((3, 2, 128, 128), F32),
-            vmem((3, 2, 128, 128), F32),
+            vmem((3, 2, 128, 128), I32),
+            vmem((3, 4, 2, 128, 128), F32),
+            vmem((2, 3, 8, 128), F32),
+            vmem((3, 4, 8, 128), F32),
             vmem((1, 256), I32),
             vmem((2, 128, 128), F32),
             vmem((2, 128, 128), F32),
@@ -476,6 +559,7 @@
             vmem((15, 16, 128), F32),
             dma((16,)), dma((2,)), dma((7,)), dma((7,)), dma(()), dma(()),
             dma((t,)), dma((t,)),
+            dma((3,)), dma((3,)), dma((3,)), dma((3,)),
             dma((t,)), dma((t,)), dma((t,)), dma((t,)), dma((t,)), dma((t,)), dma((t,)), dma((t,)),
             dma((t,)), dma((t,)),
             dma(()), dma(()), dma(()), dma(()), dma((3,)), dma((3,)), dma(()), dma(()),

time: 77.7 us -> 76.2 us (0.981)
  Pallas kernels: 73.8 us -> 72.3 us
    pallas_call x1, Pallas kernels: 73.8 us -> 72.3 us  [body(): pl.pallas_call(kernel, out_shape=(jax.ShapeDtypeStruct((256, 128), F32),...]
where the time goes in v4:
time: 76.2 us; the launch traced here: 76.1 us
  Pallas kernels  72.3 us (95%)
  local copies, waits for them, and re-layouts  3.14 us (4%)
    pallas_call x1, Pallas kernels, body(): pl.pallas_call(kernel, out_shape=(jax.ShapeDtypeStruct((256, 128), F32),...  72.3 us
    unnamed x6, local copies, waits for them, and re-layouts  3.14 us

profile of v4, /device:TPU:1, one launch (start us, length us, event | category | flops | bytes accessed | tf_op | source)
XLA Modules:
  0.0 76.1 jit_solution(16203381966959289994)
XLA Ops:
  0.6 0.0 copy-start
  0.6 0.8 %copy-done = s32[16384]{0:T(1024)S(1)} copy-done((s32[16384]{0:T(1024)S(1)}, s32[16384]{0:T(1024)}, u32[]{:S(2)}) %copy-start) | copy-done | bytes 65560
  1.5 0.0 copy-start.1
  1.5 0.7 copy-done.1
  2.1 72.3 %shard_map.50 = (f32[256,128]{1,0:T(8,128)S(1)}, f32[4,4,8,16,128]{4,3,2,1,0:T(8,128)S(1)}) custom-call(f32[16,8,128,128]{3,2,1,0:T(8,128)} %bitcast.7, s32[128,128]{1,0:T(8,128)S(1)} %bitcast.5, s32[2,128]{1,0:T(2,128)S(1)} %bitcast.6), custom_call_target="tpu_custom_call" | custom-call | tf_op jit(solution)/shard_map/pallas_call | solution.py:524
  74.4 0.7 copy.7
  75.1 1.0 %copy.8 = f32[16,128,128]{2,1,0:T(8,128)} copy(f32[16,128,128]{2,1,0:T(8,128)S(1)} %bitcast.4) | data formatting | bytes 2097152
Async XLA Ops:
  0.6 0.8 %copy-start = (s32[16384]{0:T(1024)S(1)}, s32[16384]{0:T(1024)}, u32[]{:S(2)}) copy-start(s32[16384]{0:T(1024)} %param.4) | copy-start | bytes 196612
  1.5 0.7 copy-start.1

commit v5 on v4

--- a/solution.py
+++ b/solution.py
@@ -51,11 +51,11 @@
 
 def kernel(
     matrix_ref, signs_ref, samples_ref, sketch_ref, factors_ref,
-    X, SIB, P1, R1, R2, R3, R4, T3, R5, Y8, IDX, SGN, SMP, ML, OW, EB, FT, ET, POS, WF, WALL, G, RG1, RG2, GF, OUT, DUM,
+    X, SIB, P1, R1, R2, R3, R4, T3, R5, Y8, IDX, SGN, SMP, ML, OW, EB, FT, ET, POS, WF, WALL, G, RG1, RG2, GF, DUM,
     load_sem, in_sem, y_send, y_recv, p_send, p_recv, sib_send, sib_recv,
     e_send, e_recv, x_send, x_recv, s1, r1, s2, r2, s3, r3, s4, r4, s5, r5,
     w_send, w_recv, g1_send, g1_recv, g2_send, g2_recv, g3_send, g3_recv,
-    o_send, o_recv, f_send, f_recv, out_sem,
+    o_send, o_recv, f_send, f_recv,
 ):
     me = lax.axis_index("rows")
     core = me % 2
@@ -165,7 +165,7 @@
     pl.semaphore_wait(barrier, 22)
     for n, (dy, dc) in enumerate(group):
         send(Y8.at[mine8], Y8.at[mine8], y_send.at[n], y_recv.at[n], mate(dy, dc))
-    lax.fori_loop(4, 10, front, 0, unroll=2)
+    lax.fori_loop(4, 14, front, 0, unroll=2)
     for n in range(7):
         wait(Y8.at[0], y_recv.at[n])
     for q in range(8):
@@ -173,7 +173,7 @@
             IDX[z_pos, x_pos, j, q : q + 1, :] = Y8[q, j : j + 1, :]
     for dz, dx in plane:
         send(IDX.at[z_pos, x_pos], IDX.at[z_pos, x_pos], p_send, p_recv, peer(dz, dx))
-    lax.fori_loop(10, 16, front, 0, unroll=2)
+    lax.fori_loop(14, 16, front, 0, unroll=2)
 
     def second(step):
         def tile_step(tile, carry):
@@ -397,7 +397,7 @@
                     send(FT.at[((a + hop) % 4) // 2, s], ET.at[s, a], x_send.at[s], x_recv.at[s], along(stride, hop))
                 ET[s, a] = FT[a // 2, s]
         each(work, EARLY, TICKS, everything)
-        if work is make:
+        if work is first_pass:
             lax.fori_loop(0, 3, produce_early, 0)
 
     for s in range(3):
@@ -459,8 +459,8 @@
 
         @pl.when(core == r % 2)
         def _():
-            OUT[z_pos, x_pos, r] = panel
-            block = OUT.at[z_pos, x_pos, r]
+            factors_ref[z_pos, x_pos, r] = panel
+            block = factors_ref.at[z_pos, x_pos, r]
             for dz, dx in plane:
                 send(block, block, o_send.at[r // 2], o_recv.at[r // 2], peer(dz, dx))
 
@@ -471,30 +471,18 @@
             work = work[16:] - dot_tt(lhs, rhs)[16 * r + 16 :]
 
     def share(n):
-        slab = OUT.at[:, :, 2 * n + core]
+        slab = factors_ref.at[:, :, 2 * n + core]
         wait(DUM, o_recv.at[n])
         send(slab, slab, f_send.at[n], f_recv.at[n], sibling)
-        return pltpu.make_async_copy(slab, factors_ref.at[:, :, 2 * n + core], out_sem.at[n])
-
-    def store(n):
-        return pltpu.make_async_copy(
-            OUT.at[:, :, 2 * n + 1 - core], factors_ref.at[:, :, 2 * n + 1 - core], out_sem.at[4 + n]
-        )
-
-    for n in range(4):
-        share(n).start()
-    for n in range(4):
-        wait(OUT.at[:, :, 0], f_recv.at[n])
-        store(n).start()
+
+    for n in range(2):
+        share(n)
 
     for n in range(7):
         wait(Y8.at[0], y_send.at[n])
     wait(DUM, p_send)
     for n in range(3):
         wait(RG2.at[0], g2_send.at[n])
-    for n in range(4):
-        wait(DUM, o_send.at[n])
-        wait(OUT.at[:, :, 0], f_send.at[n])
     wait(GF.at[0], g3_send)
     wait(RG1, g1_send)
     wait(WALL.at[0], w_send)
@@ -513,8 +501,14 @@
 
     each(sent, 0, EARLY, late)
     each(sent, EARLY, TICKS, everything)
-    for n in range(8):
-        wait(OUT.at[:, :, 0], out_sem.at[n])
+
+    for n in range(2, 4):
+        share(n)
+    for n in range(4):
+        wait(factors_ref.at[:, :, 0], f_recv.at[n])
+    for n in range(4):
+        wait(DUM, o_send.at[n])
+        wait(factors_ref.at[:, :, 0], f_send.at[n])
 
 
 def body(matrix, signs, samples):
@@ -528,7 +522,7 @@
             jax.ShapeDtypeStruct((4, 4, 8, 16, 128), F32),
         ),
         in_specs=[pl.BlockSpec(memory_space=pltpu.HBM)] * 3,
-        out_specs=(pl.BlockSpec(memory_space=pltpu.VMEM), pl.BlockSpec(memory_space=pl.ANY)),
+        out_specs=(pl.BlockSpec(memory_space=pltpu.VMEM), pl.BlockSpec(memory_space=pltpu.VMEM)),
         scratch_shapes=[
             vmem((16, 8, 128, 128), F32),
             vmem((8, 8, 128, 128), F32),
@@ -555,7 +549,6 @@
             vmem((64, 128), F32),
             vmem((3, 64, 128), F32),
             vmem((2, 64, 128), F32),
-            vmem((4, 4, 8, 16, 128), F32),
             vmem((15, 16, 128), F32),
             dma((16,)), dma((2,)), dma((7,)), dma((7,)), dma(()), dma(()),
             dma((t,)), dma((t,)),
@@ -563,7 +556,7 @@
             dma((t,)), dma((t,)), dma((t,)), dma((t,)), dma((t,)), dma((t,)), dma((t,)), dma((t,)),
             dma((t,)), dma((t,)),
             dma(()), dma(()), dma(()), dma(()), dma((3,)), dma((3,)), dma(()), dma(()),
-            dma((4,)), dma((4,)), dma((4,)), dma((4,)), dma((8,)),
+            dma((4,)), dma((4,)), dma((4,)), dma((4,)),
         ],
         compiler_params=pltpu.CompilerParams(
             collective_id=0, has_side_effects=True, vmem_limit_bytes=48 * 1024 * 1024

time: 76.2 us -> 75.3 us (0.988)
  Pallas kernels: 72.3 us -> 71.3 us
    pallas_call x1, Pallas kernels: 72.3 us -> 71.3 us  [body(): pl.pallas_call(kernel, out_shape=(jax.ShapeDtypeStruct((256, 128), F32),...]
where the time goes in v5:
time: 75.3 us; the launch traced here: 75.1 us
  Pallas kernels  71.3 us (95%)
  local copies, waits for them, and re-layouts  3.14 us (4%)
    pallas_call x1, Pallas kernels, body(): pl.pallas_call(kernel, out_shape=(jax.ShapeDtypeStruct((256, 128), F32),...  71.3 us
    unnamed x6, local copies, waits for them, and re-layouts  3.14 us

profile of v5, /device:TPU:1, one launch (start us, length us, event | category | flops | bytes accessed | tf_op | source)
XLA Modules:
  0.0 75.1 jit_solution(1485556324925356532)
XLA Ops:
  0.6 0.0 copy-start
  0.6 0.8 %copy-done = s32[16384]{0:T(1024)S(1)} copy-done((s32[16384]{0:T(1024)S(1)}, s32[16384]{0:T(1024)}, u32[]{:S(2)}) %copy-start) | copy-done | bytes 65560
  1.5 0.0 copy-start.1
  1.5 0.7 copy-done.1
  2.1 71.3 %shard_map.50 = (f32[256,128]{1,0:T(8,128)S(1)}, f32[4,4,8,16,128]{4,3,2,1,0:T(8,128)S(1)}) custom-call(f32[16,8,128,128]{3,2,1,0:T(8,128)} %bitcast.7, s32[128,128]{1,0:T(8,128)S(1)} %bitcast.5, s32[2,128]{1,0:T(2,128)S(1)} %bitcast.6), custom_call_target="tpu_custom_call" | custom-call | tf_op jit(solution)/shard_map/pallas_call | solution.py:518
  73.5 0.7 copy.7
  74.2 1.0 %copy.8 = f32[16,128,128]{2,1,0:T(8,128)} copy(f32[16,128,128]{2,1,0:T(8,128)S(1)} %bitcast.4) | data formatting | bytes 2097152
Async XLA Ops:
  0.6 0.8 %copy-start = (s32[16384]{0:T(1024)S(1)}, s32[16384]{0:T(1024)}, u32[]{:S(2)}) copy-start(s32[16384]{0:T(1024)} %param.4) | copy-start | bytes 196612
  1.5 0.7 copy-start.1

commit v6 on v5

--- a/solution.py
+++ b/solution.py
@@ -50,9 +50,9 @@
 
 
 def kernel(
-    matrix_ref, signs_ref, samples_ref, sketch_ref, factors_ref,
-    X, SIB, P1, R1, R2, R3, R4, T3, R5, Y8, IDX, SGN, SMP, ML, OW, EB, FT, ET, POS, WF, WALL, G, RG1, RG2, GF, DUM,
-    load_sem, in_sem, y_send, y_recv, p_send, p_recv, sib_send, sib_recv,
+    matrix_ref, small_ref, sketch_ref, factors_ref,
+    X, SIB, P1, R1, R2, R3, R4, T3, R5, Y8, IDX, ML, OW, EB, FT, ET, POS, WF, WALL, G, RG1, RG2, GF, DUM,
+    load_sem, y_send, y_recv, p_send, p_recv, sib_send, sib_recv,
     e_send, e_recv, x_send, x_recv, s1, r1, s2, r2, s3, r3, s4, r4, s5, r5,
     w_send, w_recv, g1_send, g1_recv, g2_send, g2_recv, g3_send, g3_recv,
     o_send, o_recv, f_send, f_recv,
@@ -81,10 +81,6 @@
     def load(chunk):
         return pltpu.make_async_copy(matrix_ref.at[chunk], X.at[chunk], load_sem.at[chunk])
 
-    fetch_samples = pltpu.make_async_copy(samples_ref, SMP, in_sem.at[0])
-    fetch_samples.start()
-    fetch_signs = pltpu.make_async_copy(signs_ref, SGN, in_sem.at[1])
-    fetch_signs.start()
     for chunk in range(16):
         load(chunk).start()
 
@@ -104,9 +100,8 @@
         pl.semaphore_signal(barrier, inc=1, device_id=(peer(dz, dx),), device_id_type=MESH)
 
     had = (1 - 2 * odd(iota((128, 128), 0) & iota((128, 128), 1))).astype(F32)
-    fetch_samples.wait()
-
-    samples = SMP[...]
+
+    samples = small_ref[128:130, :]
     part = (samples >> 7) & 127
     intervals = jnp.concatenate([part[0:1], part[1:2]], axis=1)
     values = jnp.concatenate([samples[0:1], samples[1:2]], axis=1)
@@ -136,7 +131,7 @@
         load(chunk).wait()
         for al in range(8):
             high, low = split2(X[chunk, al])
-            sign = SGN[pl.ds(chunk * 8 + al, 1), :].astype(F32)
+            sign = small_ref[pl.ds(chunk * 8 + al, 1), :].astype(F32)
             signed = (had * sign).astype(BF16)
             X[chunk, al] = jnp.dot(
                 jnp.concatenate([signed, signed], axis=1),
@@ -160,7 +155,6 @@
                 out[n + span] = v[n] - v[n + span]
         return out
 
-    fetch_signs.wait()
     lax.fori_loop(0, 4, front, 0, unroll=2)
     pl.semaphore_wait(barrier, 22)
     for n, (dy, dc) in enumerate(group):
@@ -515,13 +509,14 @@
     dma = pltpu.SemaphoreType.DMA
     vmem = pltpu.VMEM
     t, s = TICKS, STREAMS
+    small = jnp.concatenate([signs, samples]).reshape(130, 128)
     sketch, factors = pl.pallas_call(
         kernel,
         out_shape=(
             jax.ShapeDtypeStruct((256, 128), F32),
             jax.ShapeDtypeStruct((4, 4, 8, 16, 128), F32),
         ),
-        in_specs=[pl.BlockSpec(memory_space=pltpu.HBM)] * 3,
+        in_specs=[pl.BlockSpec(memory_space=pltpu.HBM), pl.BlockSpec(memory_space=pltpu.VMEM)],
         out_specs=(pl.BlockSpec(memory_space=pltpu.VMEM), pl.BlockSpec(memory_space=pltpu.VMEM)),
         scratch_shapes=[
             vmem((16, 8, 128, 128), F32),
@@ -535,8 +530,6 @@
             vmem((t, s, 3, 8, 128), F32),
             vmem((8, 8, 128), I32),
             vmem((4, 4, 2, 8, 128), I32),
-            vmem((128, 128), I32),
-            vmem((2, 128), I32),
             vmem((3, 2, 128, 128), I32),
             vmem((3, 2, 128, 128), I32),
             vmem((3, 4, 2, 128, 128), F32),
@@ -550,7 +543,7 @@
             vmem((3, 64, 128), F32),
             vmem((2, 64, 128), F32),
             vmem((15, 16, 128), F32),
-            dma((16,)), dma((2,)), dma((7,)), dma((7,)), dma(()), dma(()),
+            dma((16,)), dma((7,)), dma((7,)), dma(()), dma(()),
             dma((t,)), dma((t,)),
             dma((3,)), dma((3,)), dma((3,)), dma((3,)),
             dma((t,)), dma((t,)), dma((t,)), dma((t,)), dma((t,)), dma((t,)), dma((t,)), dma((t,)),
@@ -561,7 +554,7 @@
         compiler_params=pltpu.CompilerParams(
             collective_id=0, has_side_effects=True, vmem_limit_bytes=48 * 1024 * 1024
         ),
-    )(matrix.reshape(16, 8, 128, 128), signs.reshape(128, 128), samples.reshape(2, 128))
+    )(matrix.reshape(16, 8, 128, 128), small)
     return sketch, factors.reshape(16, 128, 128)
 
 

time: 75.3 us -> 74.5 us (0.989)
  local copies, waits for them, and re-layouts: 3.14 us -> 1.63 us
  other arithmetic: 0 us -> 0.86 us
    unnamed x6 -> x2, local copies, waits for them, and re-layouts: 3.14 us -> 1.63 us
    reshape x0 -> x1, other arithmetic: none -> 0.86 us  [body(): small = jnp.concatenate([signs, samples]).reshape(130, 128)]
where the time goes in v6:
time: 74.5 us; the launch traced here: 74.4 us
  Pallas kernels  71.3 us (96%)
  local copies, waits for them, and re-layouts  1.63 us (2%)
  other arithmetic  0.86 us (1%)
    pallas_call x1, Pallas kernels, body(): pl.pallas_call(kernel, out_shape=(jax.ShapeDtypeStruct((256, 128), F32),...  71.3 us
    unnamed x2, local copies, waits for them, and re-layouts  1.63 us

profile of v6, /device:TPU:1, one launch (start us, length us, event | category | flops | bytes accessed | tf_op | source)
XLA Modules:
  0.0 74.4 jit_solution(16343446626926010989)
XLA Ops:
  0.6 0.9 %add_bitcast_fusion.small_ref = s32[130,128]{1,0:T(8,128)S(1)} fusion(s32[256]{0:T(256)} %param.5, s32[16384]{0:T(1024)} %param.4), kind=kLoop, calls=%fused_computation | loop fusion | flops 16640 | bytes 133120 | tf_op jit(solution)/shard_map/reshape | solution.py:512
  1.5 71.3 %shard_map.50 = (f32[256,128]{1,0:T(8,128)S(1)}, f32[4,4,8,16,128]{4,3,2,1,0:T(8,128)S(1)}) custom-call(f32[16,8,128,128]{3,2,1,0:T(8,128)} %bitcast.5, s32[130,128]{1,0:T(8,128)S(1)} %add_bitcast_fusion.small_ref), custom_call_target="tpu_custom_call" | custom-call | tf_op jit(solution)/shard_map/pallas_call | solution.py:513
  72.8 0.7 copy.7
  73.4 1.0 %copy.8 = f32[16,128,128]{2,1,0:T(8,128)} copy(f32[16,128,128]{2,1,0:T(8,128)S(1)} %bitcast.4) | data formatting | bytes 2097152

commit v7 on v6

--- a/solution.py
+++ b/solution.py
@@ -409,12 +409,9 @@
             WF[ct, 16 * tick : 16 * tick + 16, :] = jnp.concatenate(rows, axis=0)
 
     send(WF.at[1 - core], WALL.at[core], w_send, w_recv, sibling)
-    high, mid, low = split3(WF[...].reshape(256, 128))
-    square = dot_tt(high, jnp.concatenate([high, mid], axis=1))
-    rest = dot_tt(mid, jnp.concatenate([mid, low], axis=1))
-    outer = dot_tt(high, low)
-    cross = square[:, 128:] + outer
-    gram = square[:, :128] + rest[:, :128] + (cross + cross.T)
+    high, low = split2(WF[...].reshape(256, 128))
+    square = dot_tt(high, jnp.concatenate([high, low], axis=1))
+    gram = square[:, :128] + (square[:, 128:] + square[:, 128:].T)
     G[...] = (gram * (1.0 / SAMP_OWN)).reshape(2, 64, 128)
     send(G.at[1 - core], RG1, g1_send, g1_recv, sibling)
     wait(RG1, g1_recv)

time: 74.5 us -> 74.5 us (level)
  no operation moved by 1% of the time
where the time goes in v7:
time: 74.5 us; the launch traced here: 74.3 us
  Pallas kernels  71.2 us (96%)
  local copies, waits for them, and re-layouts  1.63 us (2%)
  other arithmetic  0.86 us (1%)
    pallas_call x1, Pallas kernels, body(): pl.pallas_call(kernel, out_shape=(jax.ShapeDtypeStruct((256, 128), F32),...  71.2 us
    unnamed x2, local copies, waits for them, and re-layouts  1.63 us

profile of v7, /device:TPU:1, one launch (start us, length us, event | category | flops | bytes accessed | tf_op | source)
XLA Modules:
  0.0 74.3 jit_solution(10273357291247156444)
XLA Ops:
  0.6 0.9 %add_bitcast_fusion.small_ref = s32[130,128]{1,0:T(8,128)S(1)} fusion(s32[256]{0:T(256)} %param.5, s32[16384]{0:T(1024)} %param.4), kind=kLoop, calls=%fused_computation | loop fusion | flops 16640 | bytes 133120 | tf_op jit(solution)/shard_map/reshape | solution.py:509
  1.5 71.2 %shard_map.50 = (f32[256,128]{1,0:T(8,128)S(1)}, f32[4,4,8,16,128]{4,3,2,1,0:T(8,128)S(1)}) custom-call(f32[16,8,128,128]{3,2,1,0:T(8,128)} %bitcast.5, s32[130,128]{1,0:T(8,128)S(1)} %add_bitcast_fusion.small_ref), custom_call_target="tpu_custom_call" | custom-call | tf_op jit(solution)/shard_map/pallas_call | solution.py:510
  72.7 0.7 copy.7
  73.4 1.0 %copy.8 = f32[16,128,128]{2,1,0:T(8,128)} copy(f32[16,128,128]{2,1,0:T(8,128)S(1)} %bitcast.4) | data formatting | bytes 2097152
